TPU v7x, 512 devices: a whole 4x8x8 slice. The times are simulated.
512 devices in a mesh: seq: 32 (over z, x), tp: 16 (over y, core).
Axes of the slice: x: 4, y: 8, z: 8, core: 2. Of those that a mesh axis runs over, the one named last changes fastest.
Arguments:
- residual_in: bfloat16 [8192, 8192], P('seq', 'tp'), may hold values from -6 to 6
- features: bfloat16 [3, 8192, 8192], P(None, 'seq', 'tp'), may hold values from -6 to 6
- short_mr: float32 [3, 7, 8192], P(None, None, 'tp'), may hold values from -2 to 2
- medium: bfloat16 [128, 512], P(None, 'tp'), may hold values from -0.5 to 0.5
- skip_mr: float32 [8192], P('tp'), may hold values from 0.5 to 1.5
- li_gates: bfloat16 [2, 8192, 8192], P(None, 'seq', 'tp'), may hold values from -6 to 6
- short_li: float32 [3, 7, 8192], P(None, None, 'tp'), may hold values from -2 to 2
- poles: float32 [16, 8192], P(None, 'tp'), may hold values from 0 to 1, as said below
- residues: float32 [16, 8192], P(None, 'tp'), may hold values from -0.5 to 0.5
- skip_li: float32 [8192], P('tp'), may hold values from 0.5 to 1.5
- w_out: bfloat16 [8192, 8192], P('seq', 'tp'), may hold values from -0.0625 to 0.0625
Outputs:
- block_out: bfloat16 [8192, 8192], P('seq', 'tp')
Inputs may be any that keep to these rules, and one draw needn't show every extreme that they name: `poles`: every pole lies strictly between 0 and 1.
All inputs are finite; a program needn't handle non-finite values.
Results may differ from a plain program's by a relative error of at most 0.0064.
Values may be sent and summed in bfloat16 or wider, within the bound.
No kernel may reach another device: no remote copies, remote signals or barrier semaphores. Data moves between devices by JAX's collectives and lax.ppermute only.
A program may use at most 128 MiB of HBM per device.

v0:
```python
import jax
import jax.numpy as jnp
from jax import lax
from jax.sharding import PartitionSpec as P

block_len = 32
highest = lax.Precision.HIGHEST


def from_behind(value, axis, steps):
    count = lax.axis_size(axis)
    leading, last = (max(0, -steps), min(count, count - steps))
    return lax.ppermute(value, axis, [(source, source + steps) for source in range(leading, last)])


def short_conv(extended, tap_table):
    rim_rows = tap_table.shape[1] - 1
    tok_rows = extended.shape[1] - rim_rows
    running = jnp.zeros((extended.shape[0], tok_rows, extended.shape[2]), jnp.float32)
    for tap_lag in range(tap_table.shape[1]):
        window = extended[:, rim_rows - tap_lag : rim_rows - tap_lag + tok_rows].astype(jnp.float32)
        running = running + tap_table[:, tap_lag][:, None, :] * window
    return running


def medium_conv(extended, tap_table):
    length = tap_table.shape[0]
    tok_rows = extended.shape[0] - (length - 1)
    channels = extended.shape[1]
    groups = tap_table.shape[1]
    group_width = channels // groups
    zero_rows = jnp.zeros((length - 1, groups), tap_table.dtype)
    tap_line = jnp.concatenate([zero_rows, tap_table[::-1], zero_rows], axis=0)
    bands = jnp.stack([tap_line[length - 1 - row : 3 * length - 2 - row] for row in range(length)])
    band_head = bands[:, :length]
    band_tail = jnp.concatenate(
        [bands[:, length:], jnp.zeros((length, 1, groups), tap_table.dtype)], axis=1
    )
    padded = jnp.concatenate([extended, jnp.zeros((1, channels), extended.dtype)], axis=0)
    blocks = tok_rows // length
    win_head = padded[:tok_rows].reshape(blocks, length, groups, group_width)
    win_tail = padded[length : tok_rows + length].reshape(blocks, length, groups, group_width)
    result = jnp.einsum("ijg,bjgw->bigw", band_head, win_head, preferred_element_type=jnp.float32)
    result = result + jnp.einsum(
        "ijg,bjgw->bigw", band_tail, win_tail, preferred_element_type=jnp.float32
    )
    return result.reshape(tok_rows, channels)


def long_local(z_two, poles, residues):
    tok_rows, channels = z_two.shape
    blocks = tok_rows // block_len
    log_poles = jnp.log(poles)
    lag_steps = jnp.arange(block_len + 1).astype(jnp.float32)
    powers = jnp.exp(lag_steps[:, None, None] * log_poles[None])
    filter_taps = jnp.sum(residues[None] * powers[:block_len], axis=1)
    flipped = jnp.concatenate(
        [filter_taps[::-1], jnp.zeros((block_len - 1, channels), jnp.float32)], axis=0
    )
    toeplitz = jnp.stack(
        [flipped[block_len - 1 - row : 2 * block_len - 1 - row] for row in range(block_len)]
    )
    pieces = z_two.reshape(blocks, block_len, channels)
    inside = jnp.einsum("ijc,njc->nic", toeplitz, pieces, precision=highest)
    block_ends = jnp.einsum("jmc,njc->nmc", powers[block_len - 1 :: -1], pieces, precision=highest)
    lam_block = powers[block_len]

    def advance(carried_state, block_end):
        return (lam_block * carried_state + block_end, carried_state)

    state_end, starts = lax.scan(advance, jnp.zeros_like(lam_block), block_ends)
    mode_gain = residues[None] * powers[1:]
    across = jnp.einsum("imc,nmc->nic", mode_gain, starts, precision=highest)
    return ((inside + across).reshape(tok_rows, channels), state_end, mode_gain, log_poles)


def on_device(
    residual_in,
    features,
    short_mr,
    medium,
    skip_mr,
    li_gates,
    short_li,
    poles,
    residues,
    skip_li,
    w_out,
):
    rim_rows = short_mr.shape[1] - 1
    med_reach = medium.shape[0] - 1
    tok_rows = features.shape[1]
    channels = features.shape[2]
    tail_rows = jnp.concatenate(
        [features[:, tok_rows - rim_rows :], li_gates[:, tok_rows - rim_rows :]], axis=0
    )
    prev_rows = from_behind(tail_rows, "seq", 1)
    mr_prev = prev_rows[0:3]
    li_prev = prev_rows[3:5]
    mr_streams = short_conv(jnp.concatenate([mr_prev, features], axis=1), short_mr)
    z_one = (mr_streams[1] * mr_streams[2]).astype(jnp.bfloat16)
    z_rim = from_behind(z_one[tok_rows - med_reach :], "seq", 1)
    medium_out = medium_conv(jnp.concatenate([z_rim, z_one], axis=0), medium)
    y_one = (mr_streams[0] * (medium_out + skip_mr * z_one.astype(jnp.float32))).astype(
        jnp.bfloat16
    )
    y_prev = from_behind(y_one[tok_rows - rim_rows :], "seq", 1)
    li_front = jnp.concatenate([li_prev, y_prev[None]], axis=0)
    li_inputs = jnp.concatenate([li_gates, y_one[None]], axis=0)
    li_streams = short_conv(jnp.concatenate([li_front, li_inputs], axis=1), short_li)
    z_two = li_streams[1] * li_streams[2]
    local_out, state_end, mode_gain, log_poles = long_local(z_two, poles, residues)
    decay_dev = jnp.exp(tok_rows * log_poles)

    def relay_state(iteration, incoming_state):
        return from_behind(decay_dev * incoming_state + state_end, "seq", 1)

    incoming = lax.fori_loop(0, lax.axis_size("seq") - 1, relay_state, jnp.zeros_like(state_end))
    blocks = tok_rows // block_len
    block_starts = jnp.arange(blocks).astype(jnp.float32) * block_len
    decays = jnp.exp(block_starts[:, None, None] * log_poles[None]) * incoming[None]
    carried = jnp.einsum("imc,nmc->nic", mode_gain, decays, precision=highest).reshape(
        tok_rows, channels
    )
    long_out = local_out + carried
    y_two = (li_streams[0] * (long_out + skip_li * z_two)).astype(jnp.bfloat16)
    gathered = lax.all_gather(y_two, "tp", axis=1, tiled=True)
    projected = jnp.dot(
        gathered,
        lax.all_gather(w_out, "seq", axis=0, tiled=True),
        preferred_element_type=jnp.float32,
    )
    return (residual_in.astype(jnp.float32) + projected).astype(jnp.bfloat16)


def solution(mesh):
    placed = (
        P("seq", "tp"),
        P(None, "seq", "tp"),
        P(None, None, "tp"),
        P(None, "tp"),
        P("tp"),
        P(None, "seq", "tp"),
        P(None, None, "tp"),
        P(None, "tp"),
        P(None, "tp"),
        P("tp"),
        P("seq", "tp"),
    )
    return jax.shard_map(
        on_device, mesh=mesh, in_specs=placed, out_specs=P("seq", "tp"), check_vma=False
    )
```

profile of v0, /device:TPU:1, one launch (start us, length us, event | category | flops | bytes accessed | tf_op | source)
XLA Modules:
  0.0 745.3 jit_solution(3600436087366118464)
XLA Ops:
  134.6 27.3 %stack.614 = bf16[128,255,32]{1,0,2:T(8,128)(2,1)} concatenate(bf16[1,255,32]{1,0,2:T(2,128)(2,1)S(1)} %copy.5914, bf16[1,255,32]{1,0,2:T(2,128)(2,1)S(1)} %copy.5915, bf16[1,255,32]{1,0,2:T(2,128)(2,1)S(1)} %copy.5916, bf16[1,255,32]{1,0,2:T(2,128)(2,1)S(1)} %copy.5917, bf16[1,255,32]{1,0,2:T(2,128)(2,1)S(1)} %copy.5918, bf16[1,255,32]{1,0,2:T(2,128)(2,1)S(1)} %copy.5919, ...), dimensions={0} | concatenate | bytes 4177920 | tf_op jit(solution)/shard_map/stack | solution.py:34
  199.3 26.3 %stack.647 = f32[32,32,512]{1,0,2:T(8,128)} concatenate(f32[1,32,512]{1,0,2:T(1,128)S(1)} %copy-done.7, f32[1,32,512]{1,0,2:T(1,128)S(1)} %copy-done.8, f32[1,32,512]{1,0,2:T(1,128)S(1)} %copy-done.9, f32[1,32,512]{1,0,2:T(1,128)} %copy.6083, f32[1,32,512]{1,0,2:T(1,128)} %copy.6084, f32[1,32,512]{1,0,2:T(1,128)} %copy.6085, f32[1,32,512]{1,0,2:T(1,128)} %copy.6086, ...), dimensions={0} | concatenate | bytes 4194304 | tf_op jit(solution)/shard_map/stack | solution.py:60
  244.7 17.0 %fusion.60 = f32[512,8,32]{2,1,0:T(8,128)} fusion(f32[8,32,512]{1,0,2:T(8,128)S(1)} %copy.6111, f32[32,32,512]{1,0,2:T(8,128)} %stack.647), kind=kOutput, calls=%fused_computation.274 | convolution fusion | flops 50331648 | bytes 3145728 | tf_op jit(solution)/shard_map/ijc,njc->nic/dot_general | solution.py:64
  261.7 7.9 %convolution_bitcast_fusion = f32[8,16,512]{1,0,2:T(8,128)} fusion(f32[8,32,512]{1,0,2:T(8,128)S(1)} %copy.6111, f32[32,16,512]{0,1,2:T(8,128)S(1)} %copy-done.1), kind=kOutput, calls=%fused_computation.13 | convolution fusion | flops 25165824 | bytes 1835008 | tf_op jit(solution)/shard_map/jmc,njc->nmc/dot_general | solution.py:65
  273.3 203.6 %while.23 = (s32[]{:T(128)}, f32[16,512]{1,0:T(8,128)S(1)}, f32[16,512]{1,0:T(8,128)S(1)}, f32[16,512]{1,0:T(8,128)S(1)}, s32[]{:T(128)}) while((s32[]{:T(128)}, f32[16,512]{1,0:T(8,128)S(1)}, f32[16,512]{1,0:T(8,128)S(1)}, f32[16,512]{1,0:T(8,128)S(1)}, s32[]{:T(128)}) %tuple.244), condition=%wide.region_4.5_spmd, body=%wide.region_3.4_spmd.sunk | while | flops 16386 | bytes 262245 | solution.py:118
  293.4 5.8 collective-permute-start
  300.2 5.8 collective-permute-start
  306.9 5.9 collective-permute-start
  320.5 5.8 collective-permute-start
  334.1 5.8 collective-permute-start
  340.8 5.8 collective-permute-start
  361.2 5.8 collective-permute-start
  368.0 5.8 collective-permute-start
  374.7 5.8 collective-permute-start
  388.3 5.8 collective-permute-start
  395.1 5.8 collective-permute-start
  408.7 5.8 collective-permute-start
  415.4 5.9 collective-permute-start
  422.3 5.8 collective-permute-start
  456.3 5.8 collective-permute-start
  463.0 6.0 collective-permute-start
  492.2 132.3 %all-gather.3.cloned.1.call-done = bf16[256,8192]{1,0:T(8,128)(2,1)} async-done(((bf16[256,512]{1,0:T(8,128)(2,1)}), bf16[256,8192]{1,0:T(8,128)(2,1)}) %all-gather.3.cloned.1.call-update) | async-done | bytes 4194320 | tf_op jit(solution)/shard_map/all_gather | solution.py:127
  624.5 106.1 %all-gather.5.cloned.1.call-done = bf16[8192,512]{1,0:T(8,128)(2,1)} async-done(((bf16[256,512]{1,0:T(8,128)(2,1)}), bf16[8192,512]{1,0:T(8,128)(2,1)}) %all-gather.5.cloned.1.call-update) | async-done | bytes 8388624 | tf_op jit(solution)/shard_map/all_gather | solution.py:130
  730.6 7.7 %fusion.7 = bf16[256,512]{1,0:T(8,128)(2,1)} fusion(bf16[256,8192]{1,0:T(8,128)(2,1)} %all-gather.3.cloned.1.call-done, bf16[8192,512]{1,0:T(8,128)(2,1)} %all-gather.5.cloned.1.call-done, bf16[256,512]{1,0:T(8,128)(2,1)S(1)} %copy-done.140), kind=kOutput, calls=%fused_computation.24 | convolution fusion | flops 2147876864 | bytes 13107200 | tf_op jit(solution)/shard_map/dot_general | solution.py:128
  (627 shorter events, 312.3 us)
Async XLA Ops:
  6.5 618.0 %all-gather.3.cloned.1.call-start = ((), (), s32[]{:S(2)}) async-start(), calls=%async_computation | async-start | bytes 4456448 | tf_op jit(solution)/shard_map/all_gather | solution.py:127
  8.0 17.8 %collective-permute-start.1 = (bf16[5,6,512]{2,1,0:T(8,128)(2,1)S(1)}, bf16[5,6,512]{2,1,0:T(8,128)(2,1)S(1)}, u32[]{:S(2)}, u32[]{:S(2)}) collective-permute-start(bf16[5,6,512]{2,1,0:T(8,128)(2,1)S(1)} %pad_maximum_fusion.2), channel_id=1, source_target_pairs={{0,16},{16,32},{32,48},{48,64},{64,80},{80,96},{96,112},{112,128},... | collective-permute-start | bytes 92168 | tf_op jit(solution)/shard_map/ppermute | solution.py:13
  31.2 194.4 %collective-permute-start.2 = (bf16[127,512]{0,1:T(8,128)(2,1)}, bf16[127,512]{0,1:T(8,128)(2,1)}, u32[]{:S(2)}, u32[]{:S(2)}) collective-permute-start(bf16[127,512]{0,1:T(8,128)(2,1)} %slice_bitcast_fusion.4), channel_id=1, source_target_pairs={{0,16},{16,32},{32,48},{48,64},{64,80},{80,96},{96,112},{112,128},... | collective-permute-start | bytes 390152 | tf_op jit(solution)/shard_map/ppermute | solution.py:13
  293.4 6.8 collective-permute-start
  300.2 6.8 collective-permute-start
  306.9 6.9 collective-permute-start
  320.5 6.8 collective-permute-start
  327.3 6.8 collective-permute-start
  334.1 6.8 collective-permute-start
  340.8 6.8 collective-permute-start
  347.6 6.9 collective-permute-start
  361.2 6.8 collective-permute-start
  368.0 6.8 collective-permute-start
  374.7 6.8 collective-permute-start
  381.5 6.8 collective-permute-start
  388.3 6.8 collective-permute-start
  395.1 6.9 collective-permute-start
  408.7 6.8 collective-permute-start
  415.4 6.9 collective-permute-start
  429.1 6.8 collective-permute-start
  442.7 6.9 collective-permute-start
  456.3 6.8 collective-permute-start
  463.0 7.0 collective-permute-start
  491.4 239.2 %all-gather.5.cloned.1.call-start = ((), (), s32[]{:S(2)}) async-start(), calls=%async_computation.1 | async-start | bytes 8650752 | tf_op jit(solution)/shard_map/all_gather | solution.py:130
  (155 other events, 3811.5 us)
Sparse Core Ops, SparseCore 0:
  491.6 132.9 all-gather.2
  627.7 102.8 all-gather.4
where the time goes:
time: 756 us; the launch traced here: 745 us
  waiting for transfers between devices  273 us (36%)
  local copies, waits for them, and re-layouts  216 us (29%)
  starting transfers between devices  182 us (24%)
  matrix products  47.2 us (6%)
  between operations  15.4 us (2%)
  other arithmetic  11.8 us (2%)
    ppermute x34, starting transfers between devices, from_behind(): lax.ppermute(value, axis, [(source, source + steps) for source in range(l...  182 us
    all_gather x1, waiting for transfers between devices, on_device(): gathered = lax.all_gather(y_two, 'tp', axis=1, tiled=True)  132 us
    another operation x137, local copies, waits for them, and re-layouts, medium_conv(): jnp.stack([tap_line[length - 1 - row:3 * length - 2 - row] for row in ran...  130 us
    all_gather x1, waiting for transfers between devices, on_device(): lax.all_gather(w_out, 'seq', axis=0, tiled=True)  106 us
    another operation x34, local copies, waits for them, and re-layouts, long_local(): jnp.stack([flipped[block_len - 1 - row:2 * block_len - 1 - row] for row i...  54.6 us
    ppermute x34, waiting for transfers between devices, from_behind(): lax.ppermute(value, axis, [(source, source + steps) for source in range(l...  33.4 us
    dot_general x1, matrix products, long_local(): inside = jnp.einsum('ijc,njc->nic', toeplitz, pieces, precision=highest)  17 us
  transfers between devices with their start and end apart: 36, of which 34 were waited for; matrix products, arithmetic and copies ran while one was open for 27% of the time, Pallas kernels for 0%

commit v1 on v0

v1 whole, which is shorter than its diff:
```python
import jax
import jax.numpy as jnp
from jax import lax
from jax.experimental import pallas as pl
from jax.experimental.pallas import tpu as pltpu
from jax.sharding import PartitionSpec as P

f32 = jnp.float32
bf16 = jnp.bfloat16
LANES = 128
SEGMENTS = 8
FRONT = 144
REACH = 16


def small(mebibytes):
    return pltpu.CompilerParams(vmem_limit_bytes=int(mebibytes * 1024) * 1024)


def power(base, exponent):
    result, square = None, base
    while exponent:
        if exponent & 1:
            result = square if result is None else result * square
        exponent >>= 1
        if exponent:
            square = square * square
    return result


def bands_kernel(line_ref, out_ref):
    for group in range(out_ref.shape[0]):
        rows = jnp.broadcast_to(line_ref[group : group + 1, :], out_ref.shape[1:])
        out_ref[group] = pltpu.roll(rows, 0, 1, stride=1, stride_axis=0).astype(bf16)


def make_bands(medium):
    taps, groups = medium.shape
    line = jnp.concatenate(
        [jnp.zeros((1, groups), medium.dtype), medium[::-1], jnp.zeros((taps - 1, groups), medium.dtype)]
    )
    per_step = 8
    return pl.pallas_call(
        bands_kernel,
        grid=(groups // per_step,),
        in_specs=[pl.BlockSpec((per_step, 2 * taps), lambda i: (i, 0))],
        out_specs=pl.BlockSpec((per_step, taps, 2 * taps), lambda i: (i, 0, 0)),
        out_shape=jax.ShapeDtypeStruct((groups, taps, 2 * taps), bf16),
        compiler_params=small(8),
        name="bands",
    )(line.T.astype(f32))


def conv_rows(buffer, taps, first, count):
    total = None
    for lag in range(len(taps)):
        term = taps[lag] * buffer[pl.ds(first - lag, count), :]
        total = term if total is None else total + term
    return total


def mix_kernel(
    feat_ref, gate_ref, halo_ref, short_mr_ref, short_li_ref, skip_ref, band_ref, pole_ref,
    z_ref, q_ref, seg_ref, end_ref,
    k_buf, v_buf, s_buf, y_buf, zwin, state_buf, med_buf,
):
    tok_rows = feat_ref.shape[1]
    taps_med = band_ref.shape[1]
    groups = band_ref.shape[0]
    group_width = LANES // groups
    n_short = short_mr_ref.shape[1]
    step = 32

    def taps_of(ref, stream):
        return [ref[stream, lag : lag + 1, :] for lag in range(n_short)]

    for buf, at, stream in ((k_buf, 0, 1), (v_buf, FRONT, 2)):
        buf[0:8, :] = jnp.zeros((8, LANES), f32)
        buf[8 : 8 + FRONT, :] = halo_ref[at : at + FRONT, :].astype(f32)
        buf[8 + FRONT :, :] = feat_ref[stream].astype(f32)
    k_taps, v_taps = taps_of(short_mr_ref, 1), taps_of(short_mr_ref, 2)
    lead = 2 * taps_med - FRONT
    zwin[0:lead, :] = jnp.zeros((lead, LANES), bf16)
    for first in range(0, FRONT + tok_rows, 16):
        count = 16
        k_part = conv_rows(k_buf, k_taps, 8 + first, count)
        v_part = conv_rows(v_buf, v_taps, 8 + first, count)
        zwin[lead + first : lead + first + count, :] = (k_part * v_part).astype(bf16)

    owner = lax.broadcasted_iota(jnp.int32, (8, LANES), 1) // group_width
    masks = [owner == group for group in range(groups)]

    def pick(product, rows, start):
        for r in range(0, rows, 8):
            total = product[r : r + 8]
            for group in range(1, groups):
                total = jnp.where(masks[group], product[group * rows + r : group * rows + r + 8], total)
            med_buf[start + r : start + r + 8, :] = total

    tail = band_ref[:, taps_med - 16 :, :].reshape(groups * 16, 2 * taps_med)
    pick(jnp.dot(tail, zwin[0 : 2 * taps_med, :], preferred_element_type=f32), 16, 0)
    whole = band_ref[...].reshape(groups * taps_med, 2 * taps_med)
    for block in range(tok_rows // taps_med):
        window = zwin[taps_med * (block + 1) : taps_med * (block + 3), :]
        pick(jnp.dot(whole, window, preferred_element_type=f32), taps_med, 16 + taps_med * block)

    s_buf[0:16, :] = halo_ref[2 * FRONT : 2 * FRONT + 16, :].astype(f32)
    s_buf[16:, :] = feat_ref[0].astype(f32)
    q_taps = taps_of(short_mr_ref, 0)
    skip = skip_ref[...]
    z_last = 2 * taps_med
    q_part = conv_rows(s_buf, q_taps, 8, 8)
    z_part = zwin[z_last - 16 : z_last, :].astype(f32)[8:16]
    y_buf[0:8, :] = (q_part * (med_buf[8:16, :] + skip * z_part)).astype(bf16).astype(f32)
    for first in range(0, tok_rows, step):
        q_part = conv_rows(s_buf, q_taps, 16 + first, step)
        z_part = zwin[z_last + first : z_last + first + step, :].astype(f32)
        y_part = q_part * (med_buf[16 + first : 16 + first + step, :] + skip * z_part)
        y_buf[8 + first : 8 + first + step, :] = y_part.astype(bf16).astype(f32)

    for buf, at, stream in ((k_buf, 16, 0), (v_buf, 32, 1)):
        tail_rows = halo_ref[2 * FRONT + at : 2 * FRONT + at + 16, :].astype(f32)
        buf[0:8, :] = tail_rows[8:16]
        buf[8 : 8 + tok_rows, :] = gate_ref[stream].astype(f32)
    li_taps = [taps_of(short_li_ref, i) for i in range(3)]
    for first in range(0, tok_rows, step):
        rows = slice(first, first + step)
        q_ref[rows, :] = conv_rows(k_buf, li_taps[0], 8 + first, step)
        k_part = conv_rows(v_buf, li_taps[1], 8 + first, step)
        z_ref[rows, :] = k_part * conv_rows(y_buf, li_taps[2], 8 + first, step)

    modes = pole_ref.shape[0]
    seg_rows = tok_rows // SEGMENTS
    pole = [jnp.broadcast_to(pole_ref[m : m + 1, :], (SEGMENTS, LANES)) for m in range(modes)]
    state = [None] * modes
    for t in range(seg_rows):
        z_now = z_ref[pl.ds(t, SEGMENTS, stride=seg_rows), :]
        state = [z_now if s is None else pole[m] * s + z_now for m, s in enumerate(state)]
    for m in range(modes):
        state_buf[m * SEGMENTS : (m + 1) * SEGMENTS, :] = state[m]
    seg_decay = power(pole_ref[...], seg_rows)
    total = state_buf[pl.ds(0, modes, stride=SEGMENTS), :]
    for s in range(1, SEGMENTS):
        total = seg_decay * total + state_buf[pl.ds(s, modes, stride=SEGMENTS), :]
    seg_ref[...] = state_buf[...]
    for copy in range(end_ref.shape[0]):
        end_ref[copy] = total


def mix(features, gates, halo, short_mr, short_li, skip_mr, bands, poles, copies):
    tok_rows, channels = features.shape[1:]
    modes = poles.shape[0]
    groups = bands.shape[0]
    tiles = channels // LANES
    per_tile = groups // tiles
    taps_med = bands.shape[1]
    shapes = [
        ((tok_rows, channels), (tok_rows, LANES), lambda i: (0, i)),
        ((tok_rows, channels), (tok_rows, LANES), lambda i: (0, i)),
        ((modes * SEGMENTS, channels), (modes * SEGMENTS, LANES), lambda i: (0, i)),
        ((copies, modes, channels), (copies, modes, LANES), lambda i: (0, 0, i)),
    ]
    return pl.pallas_call(
        mix_kernel,
        grid=(tiles,),
        in_specs=[
            pl.BlockSpec((3, tok_rows, LANES), lambda i: (0, 0, i)),
            pl.BlockSpec((2, tok_rows, LANES), lambda i: (0, 0, i)),
            pl.BlockSpec((halo.shape[0], LANES), lambda i: (0, i)),
            pl.BlockSpec((3, short_mr.shape[1], LANES), lambda i: (0, 0, i)),
            pl.BlockSpec((3, short_li.shape[1], LANES), lambda i: (0, 0, i)),
            pl.BlockSpec((1, LANES), lambda i: (0, i)),
            pl.BlockSpec((per_tile, taps_med, 2 * taps_med), lambda i: (i, 0, 0)),
            pl.BlockSpec((modes, LANES), lambda i: (0, i)),
        ],
        out_specs=[pl.BlockSpec(block, index) for _, block, index in shapes],
        out_shape=[pltpu.HBM(shape, f32) for shape, _, _ in shapes],
        scratch_shapes=[
            pltpu.VMEM((8 + FRONT + tok_rows, LANES), f32),
            pltpu.VMEM((8 + FRONT + tok_rows, LANES), f32),
            pltpu.VMEM((16 + tok_rows, LANES), f32),
            pltpu.VMEM((8 + tok_rows, LANES), f32),
            pltpu.VMEM((2 * taps_med + tok_rows, LANES), bf16),
            pltpu.VMEM((modes * SEGMENTS, LANES), f32),
            pltpu.VMEM((16 + tok_rows, LANES), f32),
        ],
        compiler_params=small(16),
        name="mix",
    )(features, gates, halo, short_mr, short_li, skip_mr.reshape(1, channels), bands, poles)


def near_kernel(tok_rows, place_ref, ends_ref, pole_ref, part_ref, total_ref):
    mine = place_ref[1]
    decay = power(pole_ref[...], tok_rows)
    part = jnp.zeros(decay.shape, f32)
    total = jnp.zeros(decay.shape, f32)
    for other in range(ends_ref.shape[0]):
        end = ends_ref[other]
        part = jnp.where(other < mine, decay * part + end, part)
        total = decay * total + end
    part_ref[...] = part
    for copy in range(total_ref.shape[0]):
        total_ref[copy] = total


def near(place, ends, poles, tok_rows, copies):
    return pl.pallas_call(
        lambda *refs: near_kernel(tok_rows, *refs),
        in_specs=[
            pl.BlockSpec(memory_space=pltpu.SMEM),
            pl.BlockSpec(memory_space=pltpu.VMEM),
            pl.BlockSpec(memory_space=pltpu.VMEM),
        ],
        out_shape=[
            jax.ShapeDtypeStruct(poles.shape, f32),
            jax.ShapeDtypeStruct((copies, *poles.shape), f32),
        ],
        compiler_params=small(4),
        name="near",
    )(place, ends, poles)


def close_kernel(
    near_count, place_ref, z_ref, q_ref, seg_ref, part_ref, total_ref, pole_ref, res_ref, skip_ref,
    y_ref, state_buf, out_buf,
):
    tok_rows = z_ref.shape[0]
    modes = pole_ref.shape[0]
    seg_rows = tok_rows // SEGMENTS
    row, mine = place_ref[0], place_ref[1]
    seg_decay = power(pole_ref[...], seg_rows)
    decay = power(seg_decay, SEGMENTS)
    row_decay = power(decay, near_count)
    far = jnp.zeros(decay.shape, f32)
    for other in range(total_ref.shape[0]):
        far = jnp.where(other < row, row_decay * far + total_ref[other], far)
    for step in range(near_count - 1):
        far = jnp.where(step < mine, decay * far, far)
    start = far + part_ref[...]
    for s in range(SEGMENTS):
        state_buf[pl.ds(s, modes, stride=SEGMENTS), :] = start
        if s < SEGMENTS - 1:
            start = seg_decay * start + seg_ref[pl.ds(s, modes, stride=SEGMENTS), :]
    state = [state_buf[m * SEGMENTS : (m + 1) * SEGMENTS, :] for m in range(modes)]
    pole = [jnp.broadcast_to(pole_ref[m : m + 1, :], (SEGMENTS, LANES)) for m in range(modes)]
    gain = [jnp.broadcast_to(res_ref[m : m + 1, :], (SEGMENTS, LANES)) for m in range(modes)]
    skip = jnp.broadcast_to(skip_ref[...], (SEGMENTS, LANES))
    for t in range(seg_rows):
        rows = pl.ds(t, SEGMENTS, stride=seg_rows)
        z_now = z_ref[rows, :]
        sums = [skip * z_now, None, None, None]
        for m in range(modes):
            state[m] = pole[m] * state[m] + z_now
            term = gain[m] * state[m]
            sums[m % 4] = term if sums[m % 4] is None else sums[m % 4] + term
        out_buf[rows, :] = q_ref[rows, :] * ((sums[0] + sums[1]) + (sums[2] + sums[3]))
    y_ref[...] = out_buf[...].astype(bf16)


def close(place, z_two, q_li, seg, part, totals, poles, residues, skip_li, near_count):
    tok_rows, channels = z_two.shape
    modes = poles.shape[0]
    column = lambda rows: pl.BlockSpec((rows, LANES), lambda i: (0, i))
    return pl.pallas_call(
        lambda *refs: close_kernel(near_count, *refs),
        grid=(channels // LANES,),
        in_specs=[
            pl.BlockSpec(memory_space=pltpu.SMEM),
            column(tok_rows),
            column(tok_rows),
            column(modes * SEGMENTS),
            column(modes),
            pl.BlockSpec((totals.shape[0], modes, LANES), lambda i: (0, 0, i)),
            column(modes),
            column(modes),
            column(1),
        ],
        out_specs=column(tok_rows),
        out_shape=jax.ShapeDtypeStruct((tok_rows, channels), bf16),
        scratch_shapes=[
            pltpu.VMEM((modes * SEGMENTS, LANES), f32),
            pltpu.VMEM((tok_rows, LANES), f32),
        ],
        compiler_params=small(60.15),
        name="close",
    )(place, z_two, q_li, seg, part, totals, poles, residues, skip_li.reshape(1, channels))


def project_kernel(order, core_first, place_ref, y_ref, w_ref, *refs):
    if core_first:
        (out_ref, w_buf, sems) = refs
    else:
        (half_ref, residual_ref, out_ref, w_buf, sems) = refs
    count = y_ref.shape[0]
    copies = [
        pltpu.make_async_copy(w_ref.at[(place_ref[0] + order[k]) % count, place_ref[1]], w_buf.at[k], sems.at[k])
        for k in range(count)
    ]
    for copy in copies:
        copy.start()
    total = None
    for k in range(count):
        copies[k].wait()
        term = jnp.dot(y_ref[k], w_buf[k], preferred_element_type=f32)
        total = term if total is None else total + term
    if core_first:
        out_ref[...] = total
    else:
        out_ref[...] = (residual_ref[...].astype(f32) + (half_ref[...] + total)).astype(bf16)


def project(order, place, pieces, w_all, extra):
    count, tok_rows, depth = pieces.shape
    columns = w_all.shape[1]
    vmem = pl.BlockSpec(memory_space=pltpu.VMEM)
    return pl.pallas_call(
        lambda *refs: project_kernel(order, not extra, *refs),
        in_specs=[pl.BlockSpec(memory_space=pltpu.SMEM), vmem, pl.BlockSpec(memory_space=pltpu.HBM)]
        + [vmem] * len(extra),
        out_specs=vmem,
        out_shape=jax.ShapeDtypeStruct((tok_rows, columns), bf16 if extra else f32),
        scratch_shapes=[
            pltpu.VMEM((count, depth, columns), bf16),
            pltpu.SemaphoreType.DMA((count,)),
        ],
        cost_estimate=pl.CostEstimate(
            flops=2 * count * tok_rows * depth * columns,
            bytes_accessed=2 * count * depth * (tok_rows + columns),
            transcendentals=0,
        ),
        compiler_params=small(54),
        name="second_half" if extra else "first_half",
    )(place, pieces, w_all.reshape(count, 2, depth, columns), *extra)


def tail_kernel(feat_ref, gate_ref, out_ref, sems):
    tok_rows = feat_ref.shape[1]
    at, copies = 0, []
    for ref, stream, rows in (
        (feat_ref, 1, FRONT),
        (feat_ref, 2, FRONT),
        (feat_ref, 0, REACH),
        (gate_ref, 0, REACH),
        (gate_ref, 1, REACH),
    ):
        source = ref.at[stream, pl.ds(tok_rows - rows, rows)]
        copies.append(pltpu.make_async_copy(source, out_ref.at[pl.ds(at, rows)], sems.at[len(copies)]))
        at += rows
    for copy in copies:
        copy.start()
    for copy in copies:
        copy.wait()


def tails(features, gates):
    return pl.pallas_call(
        tail_kernel,
        in_specs=[pl.BlockSpec(memory_space=pltpu.HBM)] * 2,
        out_specs=pl.BlockSpec(memory_space=pltpu.VMEM),
        out_shape=pltpu.VMEM((2 * FRONT + 3 * REACH, features.shape[2]), bf16),
        scratch_shapes=[pltpu.SemaphoreType.DMA((5,))],
        compiler_params=small(60.15),
        name="tails",
    )(features, gates)


NEAR = 4


def on_device(
    residual_in, features, short_mr, medium, skip_mr, li_gates, short_li, poles, residues, skip_li, w_out,
):
    seq_count, tp_count = lax.axis_size("seq"), lax.axis_size("tp")
    rows_count = seq_count // NEAR
    tok_rows = features.shape[1]
    seq_at, tp_at = lax.axis_index("seq"), lax.axis_index("tp")
    place = jnp.stack([seq_at // NEAR, seq_at % NEAR]).astype(jnp.int32)

    w_all = lax.all_gather(w_out, "seq", axis=0, tiled=True)

    tail = tails(features, li_gates)
    halo = lax.ppermute(tail, "seq", [(i, i + 1) for i in range(seq_count - 1)])
    bands = make_bands(medium)
    z_two, q_li, seg, ends = mix(
        features, li_gates, halo, short_mr, short_li, skip_mr, bands, poles, NEAR
    )
    near_groups = [[row * NEAR + i for i in range(NEAR)] for row in range(rows_count)]
    far_groups = [[row * NEAR + i for row in range(rows_count)] for i in range(NEAR)]
    ends = lax.all_to_all(ends, "seq", 0, 0, tiled=True, axis_index_groups=near_groups)
    part, total = near(place, ends, poles, tok_rows, rows_count)
    totals = lax.all_to_all(total, "seq", 0, 0, tiled=True, axis_index_groups=far_groups)
    y_two = close(place, z_two, q_li, seg, part, totals, poles, residues, skip_li, NEAR)

    chips = tp_count // 2
    order = sorted(range(chips), key=lambda k: -min(k, chips - k))
    own = jnp.stack(
        [
            lax.ppermute(y_two, "tp", [((t + 2 * k) % tp_count, t) for t in range(tp_count)]) if k else y_two
            for k in order
        ]
    )
    other = lax.ppermute(own, "tp", [(t, t ^ 1) for t in range(tp_count)])
    chip_at, core_at = tp_at // 2, tp_at % 2
    here = jnp.stack([chip_at, core_at]).astype(jnp.int32)
    there = jnp.stack([chip_at, 1 - core_at]).astype(jnp.int32)
    half = project(order, here, own, w_all, ())
    return project(order, there, other, w_all, (half, residual_in))


def solution(mesh):
    placed = (
        P("seq", "tp"),
        P(None, "seq", "tp"),
        P(None, None, "tp"),
        P(None, "tp"),
        P("tp"),
        P(None, "seq", "tp"),
        P(None, None, "tp"),
        P(None, "tp"),
        P(None, "tp"),
        P("tp"),
        P("seq", "tp"),
    )
    return jax.shard_map(
        on_device, mesh=mesh, in_specs=placed, out_specs=P("seq", "tp"), check_vma=False
    )
```

time: 756 us -> 140 us (0.19); the launches traced: 745 us -> 139 us
  waiting for transfers between devices: 273 us -> 34.6 us
  local copies, waits for them, and re-layouts: 216 us -> 1.05 us
  starting transfers between devices: 182 us -> 43.2 us
  matrix products: 47.2 us -> 0 us
  Pallas kernels: 0 us -> 24.5 us
  blocking collectives: 0 us -> 21.1 us
  other arithmetic: 11.8 us -> 0.74 us
    all_gather x2 -> x1, waiting for transfers between devices: 238 us -> 0.7 us  [on_device(): w_all = lax.all_gather(w_out, 'seq', axis=0, tiled=True)]
    another operation x172 -> x1, local copies, waits for them, and re-layouts: 185 us -> 0.02 us  [on_device(): jnp.stack([lax.ppermute(y_two, 'tp', [((t + 2 * k) % tp_count, t) for t i...]
    ppermute x34 -> x9, starting transfers between devices: 182 us -> 35.6 us  [the longest x7 27 us: on_device(): lax.ppermute(y_two, 'tp', [((t + 2 * k) % tp_count, t) for t in range(tp_...]
    dot_general x7 -> x0, matrix products: 47.2 us -> none  [the longest x1 17 us: long_local(): inside = jnp.einsum('ijc,njc->nic', toeplitz, pieces, precision=highest)]
    pallas_call x0 -> x7, Pallas kernels: none -> 24.5 us  [the longest x2 10.6 us: project(): pl.pallas_call(lambda *refs: project_kernel(order, not extra, *refs), in_...]
    all_to_all x0 -> x1, blocking collectives: none -> 21.1 us  [on_device(): lax.all_to_all(total, 'seq', 0, 0, tiled=True, axis_index_groups=far_groups)]
    ppermute x34 -> x9, waiting for transfers between devices: 33.4 us -> 27.1 us  [the longest x7 25.2 us: on_device(): lax.ppermute(y_two, 'tp', [((t + 2 * k) % tp_count, t) for t in range(tp_...]
  transfers between devices with their start and end apart: 36 -> 11, of which waited for: 34 -> 8; matrix products, arithmetic and copies ran while one was open for 27% -> 1% of each run, Pallas kernels for 0% -> 14%
where the time goes in v1:
time: 140 us; the launch traced here: 139 us
  starting transfers between devices  43.2 us (31%)
  waiting for transfers between devices  34.6 us (25%)
  Pallas kernels  24.5 us (18%)
  blocking collectives  21.1 us (15%)
  between operations  13.7 us (10%)
    ppermute x7, starting transfers between devices, on_device(): lax.ppermute(y_two, 'tp', [((t + 2 * k) % tp_count, t) for t in range(tp_...  27 us
    ppermute x7, waiting for transfers between devices, on_device(): lax.ppermute(y_two, 'tp', [((t + 2 * k) % tp_count, t) for t in range(tp_...  25.2 us
    all_to_all x1, blocking collectives, on_device(): lax.all_to_all(total, 'seq', 0, 0, tiled=True, axis_index_groups=far_groups)  21.1 us
    pallas_call x2, Pallas kernels, project(): pl.pallas_call(lambda *refs: project_kernel(order, not extra, *refs), in_...  10.6 us
    all_to_all x1, starting transfers between devices, on_device(): lax.all_to_all(ends, 'seq', 0, 0, tiled=True, axis_index_groups=near_groups)  7.54 us
    pallas_call x1, Pallas kernels, mix(): pl.pallas_call(mix_kernel, grid=(tiles,), in_specs=[pl.BlockSpec((3, tok_...  6.33 us
    all_to_all x1, waiting for transfers between devices, on_device(): lax.all_to_all(ends, 'seq', 0, 0, tiled=True, axis_index_groups=near_groups)  6.15 us
    ppermute x1, starting transfers between devices, on_device(): halo = lax.ppermute(tail, 'seq', [(i, i + 1) for i in range(seq_count - 1)])  4.7 us
  transfers between devices with their start and end apart: 11, of which 8 were waited for; matrix products, arithmetic and copies ran while one was open for 1% of the time, Pallas kernels for 14%

profile of v1, /device:TPU:1, one launch (start us, length us, event | category | flops | bytes accessed | tf_op | source)
XLA Modules:
  0.0 138.9 jit_solution(13910724965444395384)
XLA Ops:
  7.3 1.8 %tails.1 = bf16[336,512]{1,0:T(8,128)(2,1)} custom-call(bf16[3,256,512]{2,1,0:T(8,128)(2,1)} %feat_ref.3, bf16[2,256,512]{2,1,0:T(8,128)(2,1)} %gate_ref.3), custom_call_target="tpu_custom_call" | custom-call | tf_op jit(solution)/shard_map/tails/pallas_call | solution.py:356
  9.1 4.7 %collective-permute-start = (bf16[336,512]{1,0:T(8,128)(2,1)}, bf16[336,512]{1,0:T(8,128)(2,1)}, u32[]{:S(2)}, u32[]{:S(2)}) collective-permute-start(bf16[336,512]{1,0:T(8,128)(2,1)} %tails.1), channel_id=1, source_target_pairs={{0,16},{16,32},{32,48},{48,64},{64,80},{80,96},{96,112},{112,128},... | collective-permute-start | bytes 1032200 | tf_op jit(solution)/shard_map/ppermute | solution.py:382
  13.8 0.8 rev.3
  14.7 0.9 bands.1.band_ref
  15.6 1.9 %collective-permute-done.halo_ref = bf16[336,512]{1,0:T(8,128)(2,1)} collective-permute-done((bf16[336,512]{1,0:T(8,128)(2,1)}, bf16[336,512]{1,0:T(8,128)(2,1)}, u32[]{:S(2)}, u32[]{:S(2)}) %collective-permute-start) | collective-permute-done | bytes 344096 | tf_op jit(solution)/shard_map/ppermute | solution.py:382
  17.6 6.3 %mix.1 = (f32[256,512]{1,0:T(8,128)}, f32[256,512]{1,0:T(8,128)}, f32[128,512]{1,0:T(8,128)}, f32[4,16,512]{2,1,0:T(8,128)}) custom-call(bf16[3,256,512]{2,1,0:T(8,128)(2,1)S(1)} %copy-done, bf16[2,256,512]{2,1,0:T(8,128)(2,1)S(1)} %copy-done.1, bf16[336,512]{1,0:T(8,128)(2,1)} %collective-permute-done.halo_ref, f32[3,7,512]{2,1,0:T(8,128)S(1)} %copy-done.3, ...), custom_call_target="tpu_custom_call" | custom-call | tf_op jit(solution)/shard_map/mix/pallas_call | solution.py:163
  23.9 7.5 %all-to-all-start = ((f32[4,16,512]{2,1,0:T(8,128)}), f32[4,16,512]{2,1,0:T(8,128)S(1)}, u32[]{:S(2)}, u32[]{:S(2)}) async-start(f32[4,16,512]{2,1,0:T(8,128)} %get-tuple-element.14), calls=%async_computation | async-start | bytes 262144 | tf_op jit(solution)/shard_map/all_to_all | solution.py:389
  31.5 6.1 %all-to-all-done.refs_1_ = f32[4,16,512]{2,1,0:T(8,128)S(1)} async-done(((f32[4,16,512]{2,1,0:T(8,128)}), f32[4,16,512]{2,1,0:T(8,128)S(1)}, u32[]{:S(2)}, u32[]{:S(2)}) %all-to-all-start) | async-done | bytes 131104 | tf_op jit(solution)/shard_map/all_to_all | solution.py:389
  38.3 21.1 %all_to_all.10.refs_5_ = f32[8,16,512]{2,1,0:T(8,128)} all-to-all(f32[8,16,512]{2,1,0:T(8,128)S(1)} %get-tuple-element.16), channel_id=1, replica_groups={{0,64,128,192,256,320,384,448},{16,80,144,208,272,336,400,464},{32,96,1..., dimensions={0} | all-to-all | bytes 524288 | tf_op jit(solution)/shard_map/all_to_all | solution.py:391
  59.4 4.3 %close.1 = bf16[256,512]{1,0:T(8,128)(2,1)} custom-call(s32[2]{0:T(128)} %copy-done.7, f32[256,512]{1,0:T(8,128)} %get-tuple-element.11.refs_1_, f32[256,512]{1,0:T(8,128)} %get-tuple-element.12.refs_2_, f32[128,512]{1,0:T(8,128)} %get-tuple-element.13.refs_3_, f32[16,512]{1,0:T(8,128)} %copy-done.5, f32[8,16,512]{2,1,0:T(8,128)} %all_to_all.10.refs_5_, ...), custom_call_target="tpu_custom_call" | custom-call | tf_op jit(solution)/shard_map/close/pallas_call | solution.py:264
  63.8 7.2 %collective-permute-start.1 = (bf16[256,512]{1,0:T(8,128)(2,1)}, bf16[256,512]{1,0:T(8,128)(2,1)S(1)}, u32[]{:S(2)}, u32[]{:S(2)}) collective-permute-start(bf16[256,512]{1,0:T(8,128)(2,1)} %close.1), channel_id=1, source_target_pairs={{8,0},{9,1},{10,2},{11,3},{12,4},{13,5},{14,6},{15,7},{0,8},{1,9},... | collective-permute-start | bytes 786440 | tf_op jit(solution)/shard_map/ppermute | solution.py:398
  71.0 2.0 %collective-permute-start.2 = (bf16[256,512]{1,0:T(8,128)(2,1)}, bf16[256,512]{1,0:T(8,128)(2,1)S(1)}, u32[]{:S(2)}, u32[]{:S(2)}) collective-permute-start(bf16[256,512]{1,0:T(8,128)(2,1)} %close.1), channel_id=1, source_target_pairs={{6,0},{7,1},{8,2},{9,3},{10,4},{11,5},{12,6},{13,7},{14,8},{15,9},... | collective-permute-start | bytes 786440 | tf_op jit(solution)/shard_map/ppermute | solution.py:398
  73.0 5.1 %collective-permute-start.3 = (bf16[256,512]{1,0:T(8,128)(2,1)}, bf16[256,512]{1,0:T(8,128)(2,1)S(1)}, u32[]{:S(2)}, u32[]{:S(2)}) collective-permute-start(bf16[256,512]{1,0:T(8,128)(2,1)} %close.1), channel_id=1, source_target_pairs={{10,0},{11,1},{12,2},{13,3},{14,4},{15,5},{0,6},{1,7},{2,8},{3,9},... | collective-permute-start | bytes 786440 | tf_op jit(solution)/shard_map/ppermute | solution.py:398
  78.1 3.3 %collective-permute-start.4 = (bf16[256,512]{1,0:T(8,128)(2,1)}, bf16[256,512]{1,0:T(8,128)(2,1)S(1)}, u32[]{:S(2)}, u32[]{:S(2)}) collective-permute-start(bf16[256,512]{1,0:T(8,128)(2,1)} %close.1), channel_id=1, source_target_pairs={{4,0},{5,1},{6,2},{7,3},{8,4},{9,5},{10,6},{11,7},{12,8},{13,9},{1... | collective-permute-start | bytes 786440 | tf_op jit(solution)/shard_map/ppermute | solution.py:398
  81.4 2.8 %collective-permute-start.5 = (bf16[256,512]{1,0:T(8,128)(2,1)}, bf16[256,512]{1,0:T(8,128)(2,1)S(1)}, u32[]{:S(2)}, u32[]{:S(2)}) collective-permute-start(bf16[256,512]{1,0:T(8,128)(2,1)} %close.1), channel_id=1, source_target_pairs={{12,0},{13,1},{14,2},{15,3},{0,4},{1,5},{2,6},{3,7},{4,8},{5,9},{6... | collective-permute-start | bytes 786440 | tf_op jit(solution)/shard_map/ppermute | solution.py:398
  84.3 4.6 %collective-permute-start.6 = (bf16[256,512]{1,0:T(8,128)(2,1)}, bf16[256,512]{1,0:T(8,128)(2,1)S(1)}, u32[]{:S(2)}, u32[]{:S(2)}) collective-permute-start(bf16[256,512]{1,0:T(8,128)(2,1)} %close.1), channel_id=1, source_target_pairs={{2,0},{3,1},{4,2},{5,3},{6,4},{7,5},{8,6},{9,7},{10,8},{11,9},{12,... | collective-permute-start | bytes 786440 | tf_op jit(solution)/shard_map/ppermute | solution.py:398
  88.9 11.0 %collective-permute-done.2 = bf16[256,512]{1,0:T(8,128)(2,1)S(1)} collective-permute-done((bf16[256,512]{1,0:T(8,128)(2,1)}, bf16[256,512]{1,0:T(8,128)(2,1)S(1)}, u32[]{:S(2)}, u32[]{:S(2)}) %collective-permute-start.2) | collective-permute-done | bytes 262176 | tf_op jit(solution)/shard_map/ppermute | solution.py:398
  99.9 1.9 %collective-permute-start.7 = (bf16[256,512]{1,0:T(8,128)(2,1)}, bf16[256,512]{1,0:T(8,128)(2,1)S(1)}, u32[]{:S(2)}, u32[]{:S(2)}) collective-permute-start(bf16[256,512]{1,0:T(8,128)(2,1)} %close.1), channel_id=1, source_target_pairs={{14,0},{15,1},{0,2},{1,3},{2,4},{3,5},{4,6},{5,7},{6,8},{7,9},{8,1... | collective-permute-start | bytes 786440 | tf_op jit(solution)/shard_map/ppermute | solution.py:398
  101.9 2.7 %collective-permute-done.3 = bf16[256,512]{1,0:T(8,128)(2,1)S(1)} collective-permute-done((bf16[256,512]{1,0:T(8,128)(2,1)}, bf16[256,512]{1,0:T(8,128)(2,1)S(1)}, u32[]{:S(2)}, u32[]{:S(2)}) %collective-permute-start.3) | collective-permute-done | bytes 262176 | tf_op jit(solution)/shard_map/ppermute | solution.py:398
  104.6 5.1 %collective-permute-done.4 = bf16[256,512]{1,0:T(8,128)(2,1)S(1)} collective-permute-done((bf16[256,512]{1,0:T(8,128)(2,1)}, bf16[256,512]{1,0:T(8,128)(2,1)S(1)}, u32[]{:S(2)}, u32[]{:S(2)}) %collective-permute-start.4) | collective-permute-done | bytes 262176 | tf_op jit(solution)/shard_map/ppermute | solution.py:398
  109.8 6.2 %collective-permute-done.6 = bf16[256,512]{1,0:T(8,128)(2,1)S(1)} collective-permute-done((bf16[256,512]{1,0:T(8,128)(2,1)}, bf16[256,512]{1,0:T(8,128)(2,1)S(1)}, u32[]{:S(2)}, u32[]{:S(2)}) %collective-permute-start.6) | collective-permute-done | bytes 262176 | tf_op jit(solution)/shard_map/ppermute | solution.py:398
  116.2 3.9 %collective-permute-start.8 = (bf16[8,256,512]{2,1,0:T(8,128)(2,1)S(1)}, bf16[8,256,512]{2,1,0:T(8,128)(2,1)}, u32[]{:S(2)}, u32[]{:S(2)}) collective-permute-start(bf16[8,256,512]{2,1,0:T(8,128)(2,1)S(1)} %bitcast_dynamic-update-slice_fusion.refs_1_), channel_id=1, source_target_pairs={{0,1},{1,0},{2,3},{3,2},{4,5},{5,4},{6,7},{7,6},{8,9},{9,8},{10,11... | collective-permute-start | bytes 6291464 | tf_op jit(solution)/shard_map/ppermute | solution.py:402
  121.4 5.3 %first_half.1.refs_3_ = f32[256,512]{1,0:T(8,128)} custom-call(s32[2]{0:T(128)} %get-tuple-element.18.refs_0_, bf16[8,256,512]{2,1,0:T(8,128)(2,1)} %copy-done.8, bf16[8,2,512,512]{3,2,1,0:T(8,128)(2,1)} %bitcast.28), custom_call_target="tpu_custom_call" | custom-call | flops 1073741824 | bytes 6291456 | tf_op jit(solution)/shard_map/first_half/pallas_call | solution.py:316
  126.7 5.3 %second_half.1 = bf16[256,512]{1,0:T(8,128)(2,1)} custom-call(s32[2]{0:T(128)} %get-tuple-element.17.refs_0_, bf16[8,256,512]{2,1,0:T(8,128)(2,1)} %collective-permute-done.8.refs_1_, bf16[8,2,512,512]{3,2,1,0:T(8,128)(2,1)} %bitcast.29, f32[256,512]{1,0:T(8,128)} %first_half.1.refs_3_, bf16[256,512]{1,0:T(8,128)(2,1)} %refs_4_.1), custom_call_target="tpu_custom_call" | custom-call | flops 1073741824 | bytes 6291456 | tf_op jit(solution)/shard_map/second_half/pallas_call | solution.py:316
  (42 shorter events, 3.1 us)
Async XLA Ops:
  6.5 11.0 %copy-start = (bf16[3,256,512]{2,1,0:T(8,128)(2,1)S(1)}, bf16[3,256,512]{2,1,0:T(8,128)(2,1)}, u32[]{:S(2)}) copy-start(bf16[3,256,512]{2,1,0:T(8,128)(2,1)} %feat_ref.3) | copy-start | bytes 2359300
  6.5 11.0 %copy-start.1 = (bf16[2,256,512]{2,1,0:T(8,128)(2,1)S(1)}, bf16[2,256,512]{2,1,0:T(8,128)(2,1)}, u32[]{:S(2)}) copy-start(bf16[2,256,512]{2,1,0:T(8,128)(2,1)} %gate_ref.3) | copy-start | bytes 1572868
  6.5 11.0 %copy-start.3 = (f32[3,7,512]{2,1,0:T(8,128)S(1)}, f32[3,7,512]{2,1,0:T(8,128)}, u32[]{:S(2)}) copy-start(f32[3,7,512]{2,1,0:T(8,128)} %short_mr_ref.1) | copy-start | bytes 129028
  6.5 11.0 %copy-start.4 = (f32[3,7,512]{2,1,0:T(8,128)S(1)}, f32[3,7,512]{2,1,0:T(8,128)}, u32[]{:S(2)}) copy-start(f32[3,7,512]{2,1,0:T(8,128)} %short_li_ref.1) | copy-start | bytes 129028
  6.5 11.0 %copy-start.6 = (f32[512]{0:T(512)S(1)}, f32[512]{0:T(512)}, u32[]{:S(2)}) copy-start(f32[512]{0:T(512)} %param.15) | copy-start | bytes 6148
  6.5 11.0 %copy-start.2 = (f32[16,512]{1,0:T(8,128)S(1)}, f32[16,512]{1,0:T(8,128)}, u32[]{:S(2)}) copy-start(f32[16,512]{1,0:T(8,128)} %refs_6_.1) | copy-start | bytes 98308
  6.6 114.9 %all-gather.2.cloned.1.call-start = ((), (), s32[]{:S(2)}) async-start(), calls=%async_computation.2 | async-start | bytes 8650752 | tf_op jit(solution)/shard_map/all_gather | solution.py:379
  9.1 8.4 %collective-permute-start = (bf16[336,512]{1,0:T(8,128)(2,1)}, bf16[336,512]{1,0:T(8,128)(2,1)}, u32[]{:S(2)}, u32[]{:S(2)}) collective-permute-start(bf16[336,512]{1,0:T(8,128)(2,1)} %tails.1), channel_id=1, source_target_pairs={{0,16},{16,32},{32,48},{48,64},{64,80},{80,96},{96,112},{112,128},... | collective-permute-start | bytes 1032200 | tf_op jit(solution)/shard_map/ppermute | solution.py:382
  23.9 13.8 %all-to-all-start = ((f32[4,16,512]{2,1,0:T(8,128)}), f32[4,16,512]{2,1,0:T(8,128)S(1)}, u32[]{:S(2)}, u32[]{:S(2)}) async-start(f32[4,16,512]{2,1,0:T(8,128)} %get-tuple-element.14), calls=%async_computation | async-start | bytes 262144 | tf_op jit(solution)/shard_map/all_to_all | solution.py:389
  31.5 27.9 %copy-start.7 = (s32[2]{0:T(128)}, s32[2]{0:T(128)S(1)}, u32[]{:S(2)}) copy-start(s32[2]{0:T(128)S(1)} %pad_add_fusion.1.refs_0_) | copy-start | bytes 28
  38.3 21.1 %copy-start.5 = (f32[16,512]{1,0:T(8,128)}, f32[16,512]{1,0:T(8,128)S(1)}, u32[]{:S(2)}) copy-start(f32[16,512]{1,0:T(8,128)S(1)} %get-tuple-element.15.refs_4_) | copy-start | bytes 98308
  63.8 52.4 %copy-start.9 = (bf16[256,512]{1,0:T(8,128)(2,1)S(1)}, bf16[256,512]{1,0:T(8,128)(2,1)}, u32[]{:S(2)}) copy-start(bf16[256,512]{1,0:T(8,128)(2,1)} %close.1) | copy-start | bytes 786436
  63.8 20.5 %collective-permute-start.1 = (bf16[256,512]{1,0:T(8,128)(2,1)}, bf16[256,512]{1,0:T(8,128)(2,1)S(1)}, u32[]{:S(2)}, u32[]{:S(2)}) collective-permute-start(bf16[256,512]{1,0:T(8,128)(2,1)} %close.1), channel_id=1, source_target_pairs={{8,0},{9,1},{10,2},{11,3},{12,4},{13,5},{14,6},{15,7},{0,8},{1,9},... | collective-permute-start | bytes 786440 | tf_op jit(solution)/shard_map/ppermute | solution.py:398
  71.0 28.9 %collective-permute-start.2 = (bf16[256,512]{1,0:T(8,128)(2,1)}, bf16[256,512]{1,0:T(8,128)(2,1)S(1)}, u32[]{:S(2)}, u32[]{:S(2)}) collective-permute-start(bf16[256,512]{1,0:T(8,128)(2,1)} %close.1), channel_id=1, source_target_pairs={{6,0},{7,1},{8,2},{9,3},{10,4},{11,5},{12,6},{13,7},{14,8},{15,9},... | collective-permute-start | bytes 786440 | tf_op jit(solution)/shard_map/ppermute | solution.py:398
  73.0 31.6 %collective-permute-start.3 = (bf16[256,512]{1,0:T(8,128)(2,1)}, bf16[256,512]{1,0:T(8,128)(2,1)S(1)}, u32[]{:S(2)}, u32[]{:S(2)}) collective-permute-start(bf16[256,512]{1,0:T(8,128)(2,1)} %close.1), channel_id=1, source_target_pairs={{10,0},{11,1},{12,2},{13,3},{14,4},{15,5},{0,6},{1,7},{2,8},{3,9},... | collective-permute-start | bytes 786440 | tf_op jit(solution)/shard_map/ppermute | solution.py:398
  78.1 31.7 %collective-permute-start.4 = (bf16[256,512]{1,0:T(8,128)(2,1)}, bf16[256,512]{1,0:T(8,128)(2,1)S(1)}, u32[]{:S(2)}, u32[]{:S(2)}) collective-permute-start(bf16[256,512]{1,0:T(8,128)(2,1)} %close.1), channel_id=1, source_target_pairs={{4,0},{5,1},{6,2},{7,3},{8,4},{9,5},{10,6},{11,7},{12,8},{13,9},{1... | collective-permute-start | bytes 786440 | tf_op jit(solution)/shard_map/ppermute | solution.py:398
  81.4 28.3 %collective-permute-start.5 = (bf16[256,512]{1,0:T(8,128)(2,1)}, bf16[256,512]{1,0:T(8,128)(2,1)S(1)}, u32[]{:S(2)}, u32[]{:S(2)}) collective-permute-start(bf16[256,512]{1,0:T(8,128)(2,1)} %close.1), channel_id=1, source_target_pairs={{12,0},{13,1},{14,2},{15,3},{0,4},{1,5},{2,6},{3,7},{4,8},{5,9},{6... | collective-permute-start | bytes 786440 | tf_op jit(solution)/shard_map/ppermute | solution.py:398
  84.3 31.7 %collective-permute-start.6 = (bf16[256,512]{1,0:T(8,128)(2,1)}, bf16[256,512]{1,0:T(8,128)(2,1)S(1)}, u32[]{:S(2)}, u32[]{:S(2)}) collective-permute-start(bf16[256,512]{1,0:T(8,128)(2,1)} %close.1), channel_id=1, source_target_pairs={{2,0},{3,1},{4,2},{5,3},{6,4},{7,5},{8,6},{9,7},{10,8},{11,9},{12,... | collective-permute-start | bytes 786440 | tf_op jit(solution)/shard_map/ppermute | solution.py:398
  99.9 16.2 %collective-permute-start.7 = (bf16[256,512]{1,0:T(8,128)(2,1)}, bf16[256,512]{1,0:T(8,128)(2,1)S(1)}, u32[]{:S(2)}, u32[]{:S(2)}) collective-permute-start(bf16[256,512]{1,0:T(8,128)(2,1)} %close.1), channel_id=1, source_target_pairs={{14,0},{15,1},{0,2},{1,3},{2,4},{3,5},{4,6},{5,7},{6,8},{7,9},{8,1... | collective-permute-start | bytes 786440 | tf_op jit(solution)/shard_map/ppermute | solution.py:398
  116.2 5.2 %copy-start.8 = (bf16[8,256,512]{2,1,0:T(8,128)(2,1)}, bf16[8,256,512]{2,1,0:T(8,128)(2,1)S(1)}, u32[]{:S(2)}) copy-start(bf16[8,256,512]{2,1,0:T(8,128)(2,1)S(1)} %bitcast_dynamic-update-slice_fusion.refs_1_) | copy-start | bytes 6291460
  116.2 10.5 %collective-permute-start.8 = (bf16[8,256,512]{2,1,0:T(8,128)(2,1)S(1)}, bf16[8,256,512]{2,1,0:T(8,128)(2,1)}, u32[]{:S(2)}, u32[]{:S(2)}) collective-permute-start(bf16[8,256,512]{2,1,0:T(8,128)(2,1)S(1)} %bitcast_dynamic-update-slice_fusion.refs_1_), channel_id=1, source_target_pairs={{0,1},{1,0},{2,3},{3,2},{4,5},{5,4},{6,7},{7,6},{8,9},{9,8},{10,11... | collective-permute-start | bytes 6291464 | tf_op jit(solution)/shard_map/ppermute | solution.py:402
Sparse Core Ops, SparseCore 0:
  10.6 110.8 all-gather.1

commit v2 on v1

--- a/solution.py
+++ b/solution.py
@@ -286,51 +286,47 @@
     )(place, z_two, q_li, seg, part, totals, poles, residues, skip_li.reshape(1, channels))
 
 
-def project_kernel(order, core_first, place_ref, y_ref, w_ref, *refs):
-    if core_first:
-        (out_ref, w_buf, sems) = refs
-    else:
-        (half_ref, residual_ref, out_ref, w_buf, sems) = refs
-    count = y_ref.shape[0]
-    copies = [
-        pltpu.make_async_copy(w_ref.at[(place_ref[0] + order[k]) % count, place_ref[1]], w_buf.at[k], sems.at[k])
-        for k in range(count)
-    ]
+def project_kernel(place_ref, own_ref, other_ref, w_ref, residual_ref, out_ref, w_buf, w_sems):
+    count = own_ref.shape[0]
+    copies = []
+    for half in range(2):
+        core = place_ref[1] if half == 0 else 1 - place_ref[1]
+        for k in range(count):
+            chip = (place_ref[0] + ORDER[k] + count) % count
+            i = half * count + k
+            copies.append(pltpu.make_async_copy(w_ref.at[chip, core], w_buf.at[i], w_sems.at[i]))
     for copy in copies:
         copy.start()
-    total = None
-    for k in range(count):
-        copies[k].wait()
-        term = jnp.dot(y_ref[k], w_buf[k], preferred_element_type=f32)
-        total = term if total is None else total + term
-    if core_first:
-        out_ref[...] = total
-    else:
-        out_ref[...] = (residual_ref[...].astype(f32) + (half_ref[...] + total)).astype(bf16)
-
-
-def project(order, place, pieces, w_all, extra):
-    count, tok_rows, depth = pieces.shape
+    total = residual_ref[...].astype(f32)
+    for i, copy in enumerate(copies):
+        y_ref = own_ref if i < count else other_ref
+        copy.wait()
+        total += jnp.dot(y_ref[i % count], w_buf[i], preferred_element_type=f32)
+    out_ref[...] = total.astype(bf16)
+
+
+def project(place, own, other, w_all, residual):
+    count, tok_rows, depth = own.shape
     columns = w_all.shape[1]
     vmem = pl.BlockSpec(memory_space=pltpu.VMEM)
-    return pl.pallas_call(
-        lambda *refs: project_kernel(order, not extra, *refs),
-        in_specs=[pl.BlockSpec(memory_space=pltpu.SMEM), vmem, pl.BlockSpec(memory_space=pltpu.HBM)]
-        + [vmem] * len(extra),
+    w_all = pltpu.with_memory_space_constraint(w_all.reshape(count, 2, depth, columns), pltpu.HBM)
+    return pl.pallas_call(
+        project_kernel,
+        in_specs=[pl.BlockSpec(memory_space=pltpu.SMEM), vmem, vmem, pl.BlockSpec(memory_space=pltpu.HBM), vmem],
         out_specs=vmem,
-        out_shape=jax.ShapeDtypeStruct((tok_rows, columns), bf16 if extra else f32),
+        out_shape=jax.ShapeDtypeStruct((tok_rows, columns), bf16),
         scratch_shapes=[
-            pltpu.VMEM((count, depth, columns), bf16),
-            pltpu.SemaphoreType.DMA((count,)),
+            pltpu.VMEM((2 * count, depth, columns), bf16),
+            pltpu.SemaphoreType.DMA((2 * count,)),
         ],
         cost_estimate=pl.CostEstimate(
-            flops=2 * count * tok_rows * depth * columns,
-            bytes_accessed=2 * count * depth * (tok_rows + columns),
+            flops=4 * count * tok_rows * depth * columns,
+            bytes_accessed=4 * count * depth * (tok_rows + columns),
             transcendentals=0,
         ),
-        compiler_params=small(54),
-        name="second_half" if extra else "first_half",
-    )(place, pieces, w_all.reshape(count, 2, depth, columns), *extra)
+        compiler_params=small(20),
+        name="project",
+    )(place, own, other, w_all, residual)
 
 
 def tail_kernel(feat_ref, gate_ref, out_ref, sems):
@@ -364,6 +360,7 @@
     )(features, gates)
 
 
+ORDER = (0, 1, -1, 2, -2, 3, -3, 4)
 NEAR = 4
 
 
@@ -391,20 +388,21 @@
     totals = lax.all_to_all(total, "seq", 0, 0, tiled=True, axis_index_groups=far_groups)
     y_two = close(place, z_two, q_li, seg, part, totals, poles, residues, skip_li, NEAR)
 
-    chips = tp_count // 2
-    order = sorted(range(chips), key=lambda k: -min(k, chips - k))
-    own = jnp.stack(
-        [
-            lax.ppermute(y_two, "tp", [((t + 2 * k) % tp_count, t) for t in range(tp_count)]) if k else y_two
-            for k in order
-        ]
-    )
+    up = [((t + 2) % tp_count, t) for t in range(tp_count)]
+    down = [((t - 2) % tp_count, t) for t in range(tp_count)]
+    ahead, behind = y_two, y_two
+    pieces = {0: y_two}
+    for step in range(1, tp_count // 4 + 1):
+        ahead = lax.ppermute(ahead, "tp", up)
+        pieces[step] = ahead
+        if step < tp_count // 4:
+            behind = lax.ppermute(behind, "tp", down)
+            pieces[-step] = behind
+    own = jnp.stack([pieces[k] for k in ORDER])
     other = lax.ppermute(own, "tp", [(t, t ^ 1) for t in range(tp_count)])
-    chip_at, core_at = tp_at // 2, tp_at % 2
-    here = jnp.stack([chip_at, core_at]).astype(jnp.int32)
-    there = jnp.stack([chip_at, 1 - core_at]).astype(jnp.int32)
-    half = project(order, here, own, w_all, ())
-    return project(order, there, other, w_all, (half, residual_in))
+    other = pltpu.with_memory_space_constraint(other, pltpu.VMEM)
+    here = jnp.stack([tp_at // 2, tp_at % 2]).astype(jnp.int32)
+    return project(here, own, other, w_all, residual_in)
 
 
 def solution(mesh):

time: 140 us -> 136 us (0.971)
  waiting for transfers between devices: 34.6 us -> 28.2 us
  starting transfers between devices: 43.2 us -> 49.1 us
  Pallas kernels: 24.5 us -> 20.5 us
    ppermute x7, waiting for transfers between devices: 25.2 us -> 9.32 us  [the longest x4 8.37 us: on_device(): ahead = lax.ppermute(ahead, 'tp', up)]
    ppermute x1, starting transfers between devices: 3.91 us -> 10.5 us  [on_device(): other = lax.ppermute(own, 'tp', [(t, t ^ 1) for t in range(tp_count)])]
    all_gather x1, waiting for transfers between devices: 0.7 us -> 6.37 us  [on_device(): w_all = lax.all_gather(w_out, 'seq', axis=0, tiled=True)]
    pallas_call x2 -> x1, Pallas kernels: 10.6 us -> 6.6 us  [project(): pl.pallas_call(project_kernel, in_specs=[pl.BlockSpec(memory_space=pltpu....]
    ppermute x1, waiting for transfers between devices: 0.01 us -> 3.8 us  [on_device(): other = lax.ppermute(own, 'tp', [(t, t ^ 1) for t in range(tp_count)])]
  transfers between devices with their start and end apart: 11 -> 11, of which waited for: 8 -> 11; matrix products, arithmetic and copies ran while one was open for 1% -> 2% of each run, Pallas kernels for 14% -> 10%
where the time goes in v2:
time: 136 us; the launch traced here: 135 us
  starting transfers between devices  49.1 us (36%)
  waiting for transfers between devices  28.2 us (21%)
  blocking collectives  21.1 us (16%)
  Pallas kernels  20.5 us (15%)
  between operations  13.6 us (10%)
  local copies, waits for them, and re-layouts  2.01 us (1%)
    all_to_all x1, blocking collectives, on_device(): lax.all_to_all(total, 'seq', 0, 0, tiled=True, axis_index_groups=far_groups)  21.1 us
    ppermute x4, starting transfers between devices, on_device(): ahead = lax.ppermute(ahead, 'tp', up)  20.5 us
    ppermute x1, starting transfers between devices, on_device(): other = lax.ppermute(own, 'tp', [(t, t ^ 1) for t in range(tp_count)])  10.5 us
    ppermute x4, waiting for transfers between devices, on_device(): ahead = lax.ppermute(ahead, 'tp', up)  8.37 us
    all_to_all x1, starting transfers between devices, on_device(): lax.all_to_all(ends, 'seq', 0, 0, tiled=True, axis_index_groups=near_groups)  7.54 us
    pallas_call x1, Pallas kernels, project(): pl.pallas_call(project_kernel, in_specs=[pl.BlockSpec(memory_space=pltpu....  6.6 us
    all_gather x1, waiting for transfers between devices, on_device(): w_all = lax.all_gather(w_out, 'seq', axis=0, tiled=True)  6.37 us
    pallas_call x1, Pallas kernels, mix(): pl.pallas_call(mix_kernel, grid=(tiles,), in_specs=[pl.BlockSpec((3, tok_...  6.33 us
  transfers between devices with their start and end apart: 11, of which 11 were waited for; matrix products, arithmetic and copies ran while one was open for 2% of the time, Pallas kernels for 10%

profile of v2, /device:TPU:1, one launch (start us, length us, event | category | flops | bytes accessed | tf_op | source)
XLA Modules:
  0.0 134.8 jit_solution(3220402513349174458)
XLA Ops:
  7.3 1.8 %tails.1 = bf16[336,512]{1,0:T(8,128)(2,1)} custom-call(bf16[3,256,512]{2,1,0:T(8,128)(2,1)} %feat_ref.3, bf16[2,256,512]{2,1,0:T(8,128)(2,1)} %gate_ref.3), custom_call_target="tpu_custom_call" | custom-call | tf_op jit(solution)/shard_map/tails/pallas_call | solution.py:352
  9.1 4.7 %collective-permute-start = (bf16[336,512]{1,0:T(8,128)(2,1)}, bf16[336,512]{1,0:T(8,128)(2,1)}, u32[]{:S(2)}, u32[]{:S(2)}) collective-permute-start(bf16[336,512]{1,0:T(8,128)(2,1)} %tails.1), channel_id=1, source_target_pairs={{0,16},{16,32},{32,48},{48,64},{64,80},{80,96},{96,112},{112,128},... | collective-permute-start | bytes 1032200 | tf_op jit(solution)/shard_map/ppermute | solution.py:379
  14.7 0.9 bands.1.band_ref
  15.6 1.9 %collective-permute-done.halo_ref = bf16[336,512]{1,0:T(8,128)(2,1)} collective-permute-done((bf16[336,512]{1,0:T(8,128)(2,1)}, bf16[336,512]{1,0:T(8,128)(2,1)}, u32[]{:S(2)}, u32[]{:S(2)}) %collective-permute-start) | collective-permute-done | bytes 344096 | tf_op jit(solution)/shard_map/ppermute | solution.py:379
  17.6 6.3 %mix.1 = (f32[256,512]{1,0:T(8,128)}, f32[256,512]{1,0:T(8,128)}, f32[128,512]{1,0:T(8,128)}, f32[4,16,512]{2,1,0:T(8,128)}) custom-call(bf16[3,256,512]{2,1,0:T(8,128)(2,1)S(1)} %copy-done, bf16[2,256,512]{2,1,0:T(8,128)(2,1)S(1)} %copy-done.1, bf16[336,512]{1,0:T(8,128)(2,1)} %collective-permute-done.halo_ref, f32[3,7,512]{2,1,0:T(8,128)S(1)} %copy-done.4, ...), custom_call_target="tpu_custom_call" | custom-call | tf_op jit(solution)/shard_map/mix/pallas_call | solution.py:163
  23.9 7.5 %all-to-all-start = ((f32[4,16,512]{2,1,0:T(8,128)}), f32[4,16,512]{2,1,0:T(8,128)S(1)}, u32[]{:S(2)}, u32[]{:S(2)}) async-start(f32[4,16,512]{2,1,0:T(8,128)} %get-tuple-element.14), calls=%async_computation | async-start | bytes 262144 | tf_op jit(solution)/shard_map/all_to_all | solution.py:386
  31.5 6.2 %all-to-all-done.refs_1_ = f32[4,16,512]{2,1,0:T(8,128)S(1)} async-done(((f32[4,16,512]{2,1,0:T(8,128)}), f32[4,16,512]{2,1,0:T(8,128)S(1)}, u32[]{:S(2)}, u32[]{:S(2)}) %all-to-all-start) | async-done | bytes 131104 | tf_op jit(solution)/shard_map/all_to_all | solution.py:386
  38.3 21.1 %all_to_all.10.refs_5_ = f32[8,16,512]{2,1,0:T(8,128)} all-to-all(f32[8,16,512]{2,1,0:T(8,128)S(1)} %get-tuple-element.16), channel_id=1, replica_groups={{0,64,128,192,256,320,384,448},{16,80,144,208,272,336,400,464},{32,96,1..., dimensions={0} | all-to-all | bytes 524288 | tf_op jit(solution)/shard_map/all_to_all | solution.py:388
  59.4 4.3 %close.1 = bf16[256,512]{1,0:T(8,128)(2,1)} custom-call(s32[2]{0:T(128)} %copy-done.8, f32[256,512]{1,0:T(8,128)} %get-tuple-element.11.refs_1_, f32[256,512]{1,0:T(8,128)} %get-tuple-element.12.refs_2_, f32[128,512]{1,0:T(8,128)} %get-tuple-element.13.refs_3_, f32[16,512]{1,0:T(8,128)} %copy-done.6, f32[8,16,512]{2,1,0:T(8,128)} %all_to_all.10.refs_5_, ...), custom_call_target="tpu_custom_call" | custom-call | tf_op jit(solution)/shard_map/close/pallas_call | solution.py:264
  63.8 4.8 %collective-permute-start.1 = (bf16[256,512]{1,0:T(8,128)(2,1)}, bf16[256,512]{1,0:T(8,128)(2,1)S(1)}, u32[]{:S(2)}, u32[]{:S(2)}) collective-permute-start(bf16[256,512]{1,0:T(8,128)(2,1)} %close.1), channel_id=1, source_target_pairs={{2,0},{3,1},{4,2},{5,3},{6,4},{7,5},{8,6},{9,7},{10,8},{11,9},{12,... | collective-permute-start | bytes 786440 | tf_op jit(solution)/shard_map/ppermute | solution.py:396
  68.6 1.9 %collective-permute-start.2 = (bf16[256,512]{1,0:T(8,128)(2,1)}, bf16[256,512]{1,0:T(8,128)(2,1)S(1)}, u32[]{:S(2)}, u32[]{:S(2)}) collective-permute-start(bf16[256,512]{1,0:T(8,128)(2,1)} %close.1), channel_id=1, source_target_pairs={{14,0},{15,1},{0,2},{1,3},{2,4},{3,5},{4,6},{5,7},{6,8},{7,9},{8,1... | collective-permute-start | bytes 786440 | tf_op jit(solution)/shard_map/ppermute | solution.py:399
  70.5 1.0 bitcast_dynamic-update-slice_fusion.7
  72.2 4.9 %collective-permute-start.3 = (bf16[256,512]{1,0:T(8,128)(2,1)S(1)}, bf16[256,512]{1,0:T(8,128)(2,1)S(1)}, u32[]{:S(2)}, u32[]{:S(2)}) collective-permute-start(bf16[256,512]{1,0:T(8,128)(2,1)S(1)} %collective-permute-done.1), channel_id=1, source_target_pairs={{2,0},{3,1},{4,2},{5,3},{6,4},{7,5},{8,6},{9,7},{10,8},{11,9},{12,... | collective-permute-start | bytes 786440 | tf_op jit(solution)/shard_map/ppermute | solution.py:396
  77.5 1.9 %collective-permute-start.4 = (bf16[256,512]{1,0:T(8,128)(2,1)S(1)}, bf16[256,512]{1,0:T(8,128)(2,1)S(1)}, u32[]{:S(2)}, u32[]{:S(2)}) collective-permute-start(bf16[256,512]{1,0:T(8,128)(2,1)S(1)} %collective-permute-done.2), channel_id=1, source_target_pairs={{14,0},{15,1},{0,2},{1,3},{2,4},{3,5},{4,6},{5,7},{6,8},{7,9},{8,1... | collective-permute-start | bytes 786440 | tf_op jit(solution)/shard_map/ppermute | solution.py:399
  79.4 1.2 collective-permute-done.3
  80.6 5.4 %collective-permute-start.5 = (bf16[256,512]{1,0:T(8,128)(2,1)S(1)}, bf16[256,512]{1,0:T(8,128)(2,1)S(1)}, u32[]{:S(2)}, u32[]{:S(2)}) collective-permute-start(bf16[256,512]{1,0:T(8,128)(2,1)S(1)} %collective-permute-done.3), channel_id=1, source_target_pairs={{2,0},{3,1},{4,2},{5,3},{6,4},{7,5},{8,6},{9,7},{10,8},{11,9},{12,... | collective-permute-start | bytes 786440 | tf_op jit(solution)/shard_map/ppermute | solution.py:396
  86.3 1.9 %collective-permute-start.6 = (bf16[256,512]{1,0:T(8,128)(2,1)S(1)}, bf16[256,512]{1,0:T(8,128)(2,1)S(1)}, u32[]{:S(2)}, u32[]{:S(2)}) collective-permute-start(bf16[256,512]{1,0:T(8,128)(2,1)S(1)} %collective-permute-done.4), channel_id=1, source_target_pairs={{14,0},{15,1},{0,2},{1,3},{2,4},{3,5},{4,6},{5,7},{6,8},{7,9},{8,1... | collective-permute-start | bytes 786440 | tf_op jit(solution)/shard_map/ppermute | solution.py:399
  88.3 2.0 %collective-permute-done.5 = bf16[256,512]{1,0:T(8,128)(2,1)S(1)} collective-permute-done((bf16[256,512]{1,0:T(8,128)(2,1)S(1)}, bf16[256,512]{1,0:T(8,128)(2,1)S(1)}, u32[]{:S(2)}, u32[]{:S(2)}) %collective-permute-start.5) | collective-permute-done | bytes 262176 | tf_op jit(solution)/shard_map/ppermute | solution.py:396
  90.2 5.4 %collective-permute-start.7 = (bf16[256,512]{1,0:T(8,128)(2,1)S(1)}, bf16[256,512]{1,0:T(8,128)(2,1)S(1)}, u32[]{:S(2)}, u32[]{:S(2)}) collective-permute-start(bf16[256,512]{1,0:T(8,128)(2,1)S(1)} %collective-permute-done.5), channel_id=1, source_target_pairs={{2,0},{3,1},{4,2},{5,3},{6,4},{7,5},{8,6},{9,7},{10,8},{11,9},{12,... | collective-permute-start | bytes 786440 | tf_op jit(solution)/shard_map/ppermute | solution.py:396
  96.0 4.5 %collective-permute-done.7 = bf16[256,512]{1,0:T(8,128)(2,1)S(1)} collective-permute-done((bf16[256,512]{1,0:T(8,128)(2,1)S(1)}, bf16[256,512]{1,0:T(8,128)(2,1)S(1)}, u32[]{:S(2)}, u32[]{:S(2)}) %collective-permute-start.7) | collective-permute-done | bytes 262176 | tf_op jit(solution)/shard_map/ppermute | solution.py:396
  100.6 10.5 %collective-permute-start.8 = (bf16[8,256,512]{2,1,0:T(8,128)(2,1)S(1)}, bf16[8,256,512]{2,1,0:T(8,128)(2,1)}, u32[]{:S(2)}, u32[]{:S(2)}) collective-permute-start(bf16[8,256,512]{2,1,0:T(8,128)(2,1)S(1)} %bitcast_dynamic-update-slice_fusion.own_ref), channel_id=1, source_target_pairs={{0,1},{1,0},{2,3},{3,2},{4,5},{5,4},{6,7},{7,6},{8,9},{9,8},{10,11... | collective-permute-start | bytes 6291464 | tf_op jit(solution)/shard_map/ppermute | solution.py:402
  111.2 3.8 %collective-permute-done.8.other_ref = bf16[8,256,512]{2,1,0:T(8,128)(2,1)} collective-permute-done((bf16[8,256,512]{2,1,0:T(8,128)(2,1)S(1)}, bf16[8,256,512]{2,1,0:T(8,128)(2,1)}, u32[]{:S(2)}, u32[]{:S(2)}) %collective-permute-start.8) | collective-permute-done | bytes 2097184 | tf_op jit(solution)/shard_map/ppermute | solution.py:402
  115.0 6.4 %all-gather.2.cloned.1.call-done = bf16[8192,512]{1,0:T(8,128)(2,1)} async-done(((bf16[256,512]{1,0:T(8,128)(2,1)}), bf16[8192,512]{1,0:T(8,128)(2,1)}) %all-gather.2.cloned.1.call-update) | async-done | bytes 8388624 | tf_op jit(solution)/shard_map/all_gather | solution.py:376
  121.4 6.6 %project.1 = bf16[256,512]{1,0:T(8,128)(2,1)} custom-call(s32[2]{0:T(128)S(1)} %pad_add_fusion.place_ref, bf16[8,256,512]{2,1,0:T(8,128)(2,1)S(1)} %bitcast_dynamic-update-slice_fusion.own_ref, bf16[8,256,512]{2,1,0:T(8,128)(2,1)} %collective-permute-done.8.other_ref, bf16[8,2,512,512]{3,2,1,0:T(8,128)(2,1)} %bitcast.27, bf16[256,512]{1,0:T(8,128)(2,1)S(1)} %copy-done.3), custom_call_target="tpu_custom_call" | custom-call | flops 2147483648 | bytes 12582912 | tf_op jit(solution)/shard_map/project/pallas_call | solution.py:313
  (39 shorter events, 4.2 us)
Async XLA Ops:
  6.5 11.0 %copy-start = (bf16[3,256,512]{2,1,0:T(8,128)(2,1)S(1)}, bf16[3,256,512]{2,1,0:T(8,128)(2,1)}, u32[]{:S(2)}) copy-start(bf16[3,256,512]{2,1,0:T(8,128)(2,1)} %feat_ref.3) | copy-start | bytes 2359300
  6.5 11.0 %copy-start.1 = (bf16[2,256,512]{2,1,0:T(8,128)(2,1)S(1)}, bf16[2,256,512]{2,1,0:T(8,128)(2,1)}, u32[]{:S(2)}) copy-start(bf16[2,256,512]{2,1,0:T(8,128)(2,1)} %gate_ref.3) | copy-start | bytes 1572868
  6.5 11.0 %copy-start.7 = (f32[512]{0:T(512)S(1)}, f32[512]{0:T(512)}, u32[]{:S(2)}) copy-start(f32[512]{0:T(512)} %param.15) | copy-start | bytes 6148
  6.5 11.0 %copy-start.4 = (f32[3,7,512]{2,1,0:T(8,128)S(1)}, f32[3,7,512]{2,1,0:T(8,128)}, u32[]{:S(2)}) copy-start(f32[3,7,512]{2,1,0:T(8,128)} %short_mr_ref.1) | copy-start | bytes 129028
  6.5 11.0 %copy-start.5 = (f32[3,7,512]{2,1,0:T(8,128)S(1)}, f32[3,7,512]{2,1,0:T(8,128)}, u32[]{:S(2)}) copy-start(f32[3,7,512]{2,1,0:T(8,128)} %short_li_ref.1) | copy-start | bytes 129028
  6.5 11.0 %copy-start.2 = (f32[16,512]{1,0:T(8,128)S(1)}, f32[16,512]{1,0:T(8,128)}, u32[]{:S(2)}) copy-start(f32[16,512]{1,0:T(8,128)} %refs_6_.1) | copy-start | bytes 98308
  6.6 114.8 %all-gather.2.cloned.1.call-start = ((), (), s32[]{:S(2)}) async-start(), calls=%async_computation.2 | async-start | bytes 8650752 | tf_op jit(solution)/shard_map/all_gather | solution.py:376
  9.1 8.4 %collective-permute-start = (bf16[336,512]{1,0:T(8,128)(2,1)}, bf16[336,512]{1,0:T(8,128)(2,1)}, u32[]{:S(2)}, u32[]{:S(2)}) collective-permute-start(bf16[336,512]{1,0:T(8,128)(2,1)} %tails.1), channel_id=1, source_target_pairs={{0,16},{16,32},{32,48},{48,64},{64,80},{80,96},{96,112},{112,128},... | collective-permute-start | bytes 1032200 | tf_op jit(solution)/shard_map/ppermute | solution.py:379
  23.9 13.8 %all-to-all-start = ((f32[4,16,512]{2,1,0:T(8,128)}), f32[4,16,512]{2,1,0:T(8,128)S(1)}, u32[]{:S(2)}, u32[]{:S(2)}) async-start(f32[4,16,512]{2,1,0:T(8,128)} %get-tuple-element.14), calls=%async_computation | async-start | bytes 262144 | tf_op jit(solution)/shard_map/all_to_all | solution.py:386
  31.5 27.9 %copy-start.8 = (s32[2]{0:T(128)}, s32[2]{0:T(128)S(1)}, u32[]{:S(2)}) copy-start(s32[2]{0:T(128)S(1)} %pad_add_fusion.1.refs_0_) | copy-start | bytes 28
  38.3 21.1 %copy-start.6 = (f32[16,512]{1,0:T(8,128)}, f32[16,512]{1,0:T(8,128)S(1)}, u32[]{:S(2)}) copy-start(f32[16,512]{1,0:T(8,128)S(1)} %get-tuple-element.15.refs_4_) | copy-start | bytes 98308
  63.7 57.6 %copy-start.3 = (bf16[256,512]{1,0:T(8,128)(2,1)S(1)}, bf16[256,512]{1,0:T(8,128)(2,1)}, u32[]{:S(2)}) copy-start(bf16[256,512]{1,0:T(8,128)(2,1)} %residual_ref.1) | copy-start | bytes 786436
  63.8 8.4 %collective-permute-start.1 = (bf16[256,512]{1,0:T(8,128)(2,1)}, bf16[256,512]{1,0:T(8,128)(2,1)S(1)}, u32[]{:S(2)}, u32[]{:S(2)}) collective-permute-start(bf16[256,512]{1,0:T(8,128)(2,1)} %close.1), channel_id=1, source_target_pairs={{2,0},{3,1},{4,2},{5,3},{6,4},{7,5},{8,6},{9,7},{10,8},{11,9},{12,... | collective-permute-start | bytes 786440 | tf_op jit(solution)/shard_map/ppermute | solution.py:396
  68.6 8.9 %collective-permute-start.2 = (bf16[256,512]{1,0:T(8,128)(2,1)}, bf16[256,512]{1,0:T(8,128)(2,1)S(1)}, u32[]{:S(2)}, u32[]{:S(2)}) collective-permute-start(bf16[256,512]{1,0:T(8,128)(2,1)} %close.1), channel_id=1, source_target_pairs={{14,0},{15,1},{0,2},{1,3},{2,4},{3,5},{4,6},{5,7},{6,8},{7,9},{8,1... | collective-permute-start | bytes 786440 | tf_op jit(solution)/shard_map/ppermute | solution.py:399
  72.2 8.4 %collective-permute-start.3 = (bf16[256,512]{1,0:T(8,128)(2,1)S(1)}, bf16[256,512]{1,0:T(8,128)(2,1)S(1)}, u32[]{:S(2)}, u32[]{:S(2)}) collective-permute-start(bf16[256,512]{1,0:T(8,128)(2,1)S(1)} %collective-permute-done.1), channel_id=1, source_target_pairs={{2,0},{3,1},{4,2},{5,3},{6,4},{7,5},{8,6},{9,7},{10,8},{11,9},{12,... | collective-permute-start | bytes 786440 | tf_op jit(solution)/shard_map/ppermute | solution.py:396
  77.5 8.8 %collective-permute-start.4 = (bf16[256,512]{1,0:T(8,128)(2,1)S(1)}, bf16[256,512]{1,0:T(8,128)(2,1)S(1)}, u32[]{:S(2)}, u32[]{:S(2)}) collective-permute-start(bf16[256,512]{1,0:T(8,128)(2,1)S(1)} %collective-permute-done.2), channel_id=1, source_target_pairs={{14,0},{15,1},{0,2},{1,3},{2,4},{3,5},{4,6},{5,7},{6,8},{7,9},{8,1... | collective-permute-start | bytes 786440 | tf_op jit(solution)/shard_map/ppermute | solution.py:399
  80.6 9.6 %collective-permute-start.5 = (bf16[256,512]{1,0:T(8,128)(2,1)S(1)}, bf16[256,512]{1,0:T(8,128)(2,1)S(1)}, u32[]{:S(2)}, u32[]{:S(2)}) collective-permute-start(bf16[256,512]{1,0:T(8,128)(2,1)S(1)} %collective-permute-done.3), channel_id=1, source_target_pairs={{2,0},{3,1},{4,2},{5,3},{6,4},{7,5},{8,6},{9,7},{10,8},{11,9},{12,... | collective-permute-start | bytes 786440 | tf_op jit(solution)/shard_map/ppermute | solution.py:396
  86.3 9.7 %collective-permute-start.6 = (bf16[256,512]{1,0:T(8,128)(2,1)S(1)}, bf16[256,512]{1,0:T(8,128)(2,1)S(1)}, u32[]{:S(2)}, u32[]{:S(2)}) collective-permute-start(bf16[256,512]{1,0:T(8,128)(2,1)S(1)} %collective-permute-done.4), channel_id=1, source_target_pairs={{14,0},{15,1},{0,2},{1,3},{2,4},{3,5},{4,6},{5,7},{6,8},{7,9},{8,1... | collective-permute-start | bytes 786440 | tf_op jit(solution)/shard_map/ppermute | solution.py:399
  90.2 10.3 %collective-permute-start.7 = (bf16[256,512]{1,0:T(8,128)(2,1)S(1)}, bf16[256,512]{1,0:T(8,128)(2,1)S(1)}, u32[]{:S(2)}, u32[]{:S(2)}) collective-permute-start(bf16[256,512]{1,0:T(8,128)(2,1)S(1)} %collective-permute-done.5), channel_id=1, source_target_pairs={{2,0},{3,1},{4,2},{5,3},{6,4},{7,5},{8,6},{9,7},{10,8},{11,9},{12,... | collective-permute-start | bytes 786440 | tf_op jit(solution)/shard_map/ppermute | solution.py:396
  100.6 14.4 %collective-permute-start.8 = (bf16[8,256,512]{2,1,0:T(8,128)(2,1)S(1)}, bf16[8,256,512]{2,1,0:T(8,128)(2,1)}, u32[]{:S(2)}, u32[]{:S(2)}) collective-permute-start(bf16[8,256,512]{2,1,0:T(8,128)(2,1)S(1)} %bitcast_dynamic-update-slice_fusion.own_ref), channel_id=1, source_target_pairs={{0,1},{1,0},{2,3},{3,2},{4,5},{5,4},{6,7},{7,6},{8,9},{9,8},{10,11... | collective-permute-start | bytes 6291464 | tf_op jit(solution)/shard_map/ppermute | solution.py:402
Sparse Core Ops, SparseCore 0:
  10.6 110.7 all-gather.1

commit v3 on v2

--- a/solution.py
+++ b/solution.py
@@ -286,22 +286,28 @@
     )(place, z_two, q_li, seg, part, totals, poles, residues, skip_li.reshape(1, channels))
 
 
-def project_kernel(place_ref, own_ref, other_ref, w_ref, residual_ref, out_ref, w_buf, w_sems):
+def project_kernel(place_ref, own_ref, other_ref, w_ref, residual_ref, out_ref, y_buf, w_buf, y_sems, w_sems):
     count = own_ref.shape[0]
     copies = []
-    for half in range(2):
+    for half, y_ref in enumerate((own_ref, other_ref)):
         core = place_ref[1] if half == 0 else 1 - place_ref[1]
         for k in range(count):
             chip = (place_ref[0] + ORDER[k] + count) % count
             i = half * count + k
-            copies.append(pltpu.make_async_copy(w_ref.at[chip, core], w_buf.at[i], w_sems.at[i]))
-    for copy in copies:
-        copy.start()
+            copies.append(
+                (
+                    pltpu.make_async_copy(y_ref.at[k], y_buf.at[i], y_sems.at[i]),
+                    pltpu.make_async_copy(w_ref.at[chip, core], w_buf.at[i], w_sems.at[i]),
+                )
+            )
+    for pair in copies:
+        for copy in pair:
+            copy.start()
     total = residual_ref[...].astype(f32)
-    for i, copy in enumerate(copies):
-        y_ref = own_ref if i < count else other_ref
-        copy.wait()
-        total += jnp.dot(y_ref[i % count], w_buf[i], preferred_element_type=f32)
+    for i, pair in enumerate(copies):
+        for copy in pair:
+            copy.wait()
+        total += jnp.dot(y_buf[i], w_buf[i], preferred_element_type=f32)
     out_ref[...] = total.astype(bf16)
 
 
@@ -309,14 +315,20 @@
     count, tok_rows, depth = own.shape
     columns = w_all.shape[1]
     vmem = pl.BlockSpec(memory_space=pltpu.VMEM)
-    w_all = pltpu.with_memory_space_constraint(w_all.reshape(count, 2, depth, columns), pltpu.HBM)
+    hbm = pl.BlockSpec(memory_space=pltpu.HBM)
+    arrays = [
+        pltpu.with_memory_space_constraint(value, pltpu.HBM)
+        for value in (own, other, w_all.reshape(count, 2, depth, columns))
+    ]
     return pl.pallas_call(
         project_kernel,
-        in_specs=[pl.BlockSpec(memory_space=pltpu.SMEM), vmem, vmem, pl.BlockSpec(memory_space=pltpu.HBM), vmem],
+        in_specs=[pl.BlockSpec(memory_space=pltpu.SMEM), hbm, hbm, hbm, vmem],
         out_specs=vmem,
         out_shape=jax.ShapeDtypeStruct((tok_rows, columns), bf16),
         scratch_shapes=[
+            pltpu.VMEM((2 * count, tok_rows, depth), bf16),
             pltpu.VMEM((2 * count, depth, columns), bf16),
+            pltpu.SemaphoreType.DMA((2 * count,)),
             pltpu.SemaphoreType.DMA((2 * count,)),
         ],
         cost_estimate=pl.CostEstimate(
@@ -326,7 +338,7 @@
         ),
         compiler_params=small(20),
         name="project",
-    )(place, own, other, w_all, residual)
+    )(place, *arrays, residual)
 
 
 def tail_kernel(feat_ref, gate_ref, out_ref, sems):
@@ -400,7 +412,6 @@
             pieces[-step] = behind
     own = jnp.stack([pieces[k] for k in ORDER])
     other = lax.ppermute(own, "tp", [(t, t ^ 1) for t in range(tp_count)])
-    other = pltpu.with_memory_space_constraint(other, pltpu.VMEM)
     here = jnp.stack([tp_at // 2, tp_at % 2]).astype(jnp.int32)
     return project(here, own, other, w_all, residual_in)
 

time: 136 us -> 135 us (level)
  no operation moved by 1% of the time
where the time goes in v3:
time: 135 us
  starting transfers between devices  49.1 us (36%)
  waiting for transfers between devices  28.3 us (21%)
  blocking collectives  21.1 us (16%)
  Pallas kernels  20.3 us (15%)
  between operations  13.7 us (10%)
  local copies, waits for them, and re-layouts  2.02 us (1%)
    all_to_all x1, blocking collectives, on_device(): lax.all_to_all(total, 'seq', 0, 0, tiled=True, axis_index_groups=far_groups)  21.1 us
    ppermute x4, starting transfers between devices, on_device(): ahead = lax.ppermute(ahead, 'tp', up)  20.6 us
    ppermute x1, starting transfers between devices, on_device(): other = lax.ppermute(own, 'tp', [(t, t ^ 1) for t in range(tp_count)])  10.5 us
    ppermute x4, waiting for transfers between devices, on_device(): ahead = lax.ppermute(ahead, 'tp', up)  8.43 us
    all_to_all x1, starting transfers between devices, on_device(): lax.all_to_all(ends, 'seq', 0, 0, tiled=True, axis_index_groups=near_groups)  7.54 us
    pallas_call x1, Pallas kernels, project(): pl.pallas_call(project_kernel, in_specs=[pl.BlockSpec(memory_space=pltpu....  6.41 us
    pallas_call x1, Pallas kernels, mix(): pl.pallas_call(mix_kernel, grid=(tiles,), in_specs=[pl.BlockSpec((3, tok_...  6.35 us
    all_gather x1, waiting for transfers between devices, on_device(): w_all = lax.all_gather(w_out, 'seq', axis=0, tiled=True)  6.34 us
  transfers between devices with their start and end apart: 11, of which 11 were waited for; matrix products, arithmetic and copies ran while one was open for 2% of the time, Pallas kernels for 10%

profile of v3, /device:TPU:1, one launch (start us, length us, event | category | flops | bytes accessed | tf_op | source)
XLA Modules:
  0.0 134.7 jit_solution(10131035149500435369)
XLA Ops:
  7.3 1.8 %tails.1 = bf16[336,512]{1,0:T(8,128)(2,1)} custom-call(bf16[3,256,512]{2,1,0:T(8,128)(2,1)} %feat_ref.3, bf16[2,256,512]{2,1,0:T(8,128)(2,1)} %gate_ref.3), custom_call_target="tpu_custom_call" | custom-call | tf_op jit(solution)/shard_map/tails/pallas_call | solution.py:364
  9.1 4.7 %collective-permute-start = (bf16[336,512]{1,0:T(8,128)(2,1)}, bf16[336,512]{1,0:T(8,128)(2,1)}, u32[]{:S(2)}, u32[]{:S(2)}) collective-permute-start(bf16[336,512]{1,0:T(8,128)(2,1)} %tails.1), channel_id=1, source_target_pairs={{0,16},{16,32},{32,48},{48,64},{64,80},{80,96},{96,112},{112,128},... | collective-permute-start | bytes 1032200 | tf_op jit(solution)/shard_map/ppermute | solution.py:391
  14.7 0.9 bands.1.band_ref
  15.6 1.9 %collective-permute-done.halo_ref = bf16[336,512]{1,0:T(8,128)(2,1)} collective-permute-done((bf16[336,512]{1,0:T(8,128)(2,1)}, bf16[336,512]{1,0:T(8,128)(2,1)}, u32[]{:S(2)}, u32[]{:S(2)}) %collective-permute-start) | collective-permute-done | bytes 344096 | tf_op jit(solution)/shard_map/ppermute | solution.py:391
  17.6 6.3 %mix.1 = (f32[256,512]{1,0:T(8,128)}, f32[256,512]{1,0:T(8,128)}, f32[128,512]{1,0:T(8,128)}, f32[4,16,512]{2,1,0:T(8,128)}) custom-call(bf16[3,256,512]{2,1,0:T(8,128)(2,1)S(1)} %copy-done, bf16[2,256,512]{2,1,0:T(8,128)(2,1)S(1)} %copy-done.1, bf16[336,512]{1,0:T(8,128)(2,1)} %collective-permute-done.halo_ref, f32[3,7,512]{2,1,0:T(8,128)S(1)} %copy-done.4, ...), custom_call_target="tpu_custom_call" | custom-call | tf_op jit(solution)/shard_map/mix/pallas_call | solution.py:163
  23.9 7.5 %all-to-all-start = ((f32[4,16,512]{2,1,0:T(8,128)}), f32[4,16,512]{2,1,0:T(8,128)S(1)}, u32[]{:S(2)}, u32[]{:S(2)}) async-start(f32[4,16,512]{2,1,0:T(8,128)} %get-tuple-element.14), calls=%async_computation | async-start | bytes 262144 | tf_op jit(solution)/shard_map/all_to_all | solution.py:398
  31.5 6.1 %all-to-all-done.refs_1_ = f32[4,16,512]{2,1,0:T(8,128)S(1)} async-done(((f32[4,16,512]{2,1,0:T(8,128)}), f32[4,16,512]{2,1,0:T(8,128)S(1)}, u32[]{:S(2)}, u32[]{:S(2)}) %all-to-all-start) | async-done | bytes 131104 | tf_op jit(solution)/shard_map/all_to_all | solution.py:398
  38.3 21.1 %all_to_all.10.refs_5_ = f32[8,16,512]{2,1,0:T(8,128)} all-to-all(f32[8,16,512]{2,1,0:T(8,128)S(1)} %get-tuple-element.16), channel_id=1, replica_groups={{0,64,128,192,256,320,384,448},{16,80,144,208,272,336,400,464},{32,96,1..., dimensions={0} | all-to-all | bytes 524288 | tf_op jit(solution)/shard_map/all_to_all | solution.py:400
  59.4 4.3 %close.1 = bf16[256,512]{1,0:T(8,128)(2,1)} custom-call(s32[2]{0:T(128)} %copy-done.8, f32[256,512]{1,0:T(8,128)} %get-tuple-element.11.refs_1_, f32[256,512]{1,0:T(8,128)} %get-tuple-element.12.refs_2_, f32[128,512]{1,0:T(8,128)} %get-tuple-element.13.refs_3_, f32[16,512]{1,0:T(8,128)} %copy-done.6, f32[8,16,512]{2,1,0:T(8,128)} %all_to_all.10.refs_5_, ...), custom_call_target="tpu_custom_call" | custom-call | tf_op jit(solution)/shard_map/close/pallas_call | solution.py:264
  63.7 4.8 %collective-permute-start.1 = (bf16[256,512]{1,0:T(8,128)(2,1)}, bf16[256,512]{1,0:T(8,128)(2,1)S(1)}, u32[]{:S(2)}, u32[]{:S(2)}) collective-permute-start(bf16[256,512]{1,0:T(8,128)(2,1)} %close.1), channel_id=1, source_target_pairs={{2,0},{3,1},{4,2},{5,3},{6,4},{7,5},{8,6},{9,7},{10,8},{11,9},{12,... | collective-permute-start | bytes 786440 | tf_op jit(solution)/shard_map/ppermute | solution.py:408
  68.5 1.9 %collective-permute-start.2 = (bf16[256,512]{1,0:T(8,128)(2,1)}, bf16[256,512]{1,0:T(8,128)(2,1)S(1)}, u32[]{:S(2)}, u32[]{:S(2)}) collective-permute-start(bf16[256,512]{1,0:T(8,128)(2,1)} %close.1), channel_id=1, source_target_pairs={{14,0},{15,1},{0,2},{1,3},{2,4},{3,5},{4,6},{5,7},{6,8},{7,9},{8,1... | collective-permute-start | bytes 786440 | tf_op jit(solution)/shard_map/ppermute | solution.py:411
  70.5 1.0 bitcast_dynamic-update-slice_fusion.7
  72.2 4.9 %collective-permute-start.3 = (bf16[256,512]{1,0:T(8,128)(2,1)S(1)}, bf16[256,512]{1,0:T(8,128)(2,1)S(1)}, u32[]{:S(2)}, u32[]{:S(2)}) collective-permute-start(bf16[256,512]{1,0:T(8,128)(2,1)S(1)} %collective-permute-done.1), channel_id=1, source_target_pairs={{2,0},{3,1},{4,2},{5,3},{6,4},{7,5},{8,6},{9,7},{10,8},{11,9},{12,... | collective-permute-start | bytes 786440 | tf_op jit(solution)/shard_map/ppermute | solution.py:408
  77.5 1.9 %collective-permute-start.4 = (bf16[256,512]{1,0:T(8,128)(2,1)S(1)}, bf16[256,512]{1,0:T(8,128)(2,1)S(1)}, u32[]{:S(2)}, u32[]{:S(2)}) collective-permute-start(bf16[256,512]{1,0:T(8,128)(2,1)S(1)} %collective-permute-done.2), channel_id=1, source_target_pairs={{14,0},{15,1},{0,2},{1,3},{2,4},{3,5},{4,6},{5,7},{6,8},{7,9},{8,1... | collective-permute-start | bytes 786440 | tf_op jit(solution)/shard_map/ppermute | solution.py:411
  79.4 1.2 collective-permute-done.3
  80.6 5.4 %collective-permute-start.5 = (bf16[256,512]{1,0:T(8,128)(2,1)S(1)}, bf16[256,512]{1,0:T(8,128)(2,1)S(1)}, u32[]{:S(2)}, u32[]{:S(2)}) collective-permute-start(bf16[256,512]{1,0:T(8,128)(2,1)S(1)} %collective-permute-done.3), channel_id=1, source_target_pairs={{2,0},{3,1},{4,2},{5,3},{6,4},{7,5},{8,6},{9,7},{10,8},{11,9},{12,... | collective-permute-start | bytes 786440 | tf_op jit(solution)/shard_map/ppermute | solution.py:408
  86.3 1.9 %collective-permute-start.6 = (bf16[256,512]{1,0:T(8,128)(2,1)S(1)}, bf16[256,512]{1,0:T(8,128)(2,1)S(1)}, u32[]{:S(2)}, u32[]{:S(2)}) collective-permute-start(bf16[256,512]{1,0:T(8,128)(2,1)S(1)} %collective-permute-done.4), channel_id=1, source_target_pairs={{14,0},{15,1},{0,2},{1,3},{2,4},{3,5},{4,6},{5,7},{6,8},{7,9},{8,1... | collective-permute-start | bytes 786440 | tf_op jit(solution)/shard_map/ppermute | solution.py:411
  88.3 2.0 %collective-permute-done.5 = bf16[256,512]{1,0:T(8,128)(2,1)S(1)} collective-permute-done((bf16[256,512]{1,0:T(8,128)(2,1)S(1)}, bf16[256,512]{1,0:T(8,128)(2,1)S(1)}, u32[]{:S(2)}, u32[]{:S(2)}) %collective-permute-start.5) | collective-permute-done | bytes 262176 | tf_op jit(solution)/shard_map/ppermute | solution.py:408
  90.3 5.4 %collective-permute-start.7 = (bf16[256,512]{1,0:T(8,128)(2,1)S(1)}, bf16[256,512]{1,0:T(8,128)(2,1)S(1)}, u32[]{:S(2)}, u32[]{:S(2)}) collective-permute-start(bf16[256,512]{1,0:T(8,128)(2,1)S(1)} %collective-permute-done.5), channel_id=1, source_target_pairs={{2,0},{3,1},{4,2},{5,3},{6,4},{7,5},{8,6},{9,7},{10,8},{11,9},{12,... | collective-permute-start | bytes 786440 | tf_op jit(solution)/shard_map/ppermute | solution.py:408
  96.0 4.6 %collective-permute-done.7 = bf16[256,512]{1,0:T(8,128)(2,1)S(1)} collective-permute-done((bf16[256,512]{1,0:T(8,128)(2,1)S(1)}, bf16[256,512]{1,0:T(8,128)(2,1)S(1)}, u32[]{:S(2)}, u32[]{:S(2)}) %collective-permute-start.7) | collective-permute-done | bytes 262176 | tf_op jit(solution)/shard_map/ppermute | solution.py:408
  100.6 10.5 %collective-permute-start.8 = (bf16[8,256,512]{2,1,0:T(8,128)(2,1)S(1)}, bf16[8,256,512]{2,1,0:T(8,128)(2,1)}, u32[]{:S(2)}, u32[]{:S(2)}) collective-permute-start(bf16[8,256,512]{2,1,0:T(8,128)(2,1)S(1)} %bitcast_dynamic-update-slice_fusion.own_ref), channel_id=1, source_target_pairs={{0,1},{1,0},{2,3},{3,2},{4,5},{5,4},{6,7},{7,6},{8,9},{9,8},{10,11... | collective-permute-start | bytes 6291464 | tf_op jit(solution)/shard_map/ppermute | solution.py:414
  111.3 3.8 %collective-permute-done.8.other_ref = bf16[8,256,512]{2,1,0:T(8,128)(2,1)} collective-permute-done((bf16[8,256,512]{2,1,0:T(8,128)(2,1)S(1)}, bf16[8,256,512]{2,1,0:T(8,128)(2,1)}, u32[]{:S(2)}, u32[]{:S(2)}) %collective-permute-start.8) | collective-permute-done | bytes 2097184 | tf_op jit(solution)/shard_map/ppermute | solution.py:414
  115.1 6.3 %all-gather.2.cloned.1.call-done = bf16[8192,512]{1,0:T(8,128)(2,1)} async-done(((bf16[256,512]{1,0:T(8,128)(2,1)}), bf16[8192,512]{1,0:T(8,128)(2,1)}) %all-gather.2.cloned.1.call-update) | async-done | bytes 8388624 | tf_op jit(solution)/shard_map/all_gather | solution.py:388
  121.4 6.4 %project.1 = bf16[256,512]{1,0:T(8,128)(2,1)} custom-call(s32[2]{0:T(128)S(1)} %pad_add_fusion.place_ref, bf16[8,256,512]{2,1,0:T(8,128)(2,1)} %copy-done.9, bf16[8,256,512]{2,1,0:T(8,128)(2,1)} %collective-permute-done.8.other_ref, bf16[8,2,512,512]{3,2,1,0:T(8,128)(2,1)} %bitcast.27, bf16[256,512]{1,0:T(8,128)(2,1)S(1)} %copy-done.3), custom_call_target="tpu_custom_call" | custom-call | flops 2147483648 | bytes 12582912 | tf_op jit(solution)/shard_map/project/pallas_call | solution.py:323
  (41 shorter events, 4.2 us)
Async XLA Ops:
  6.5 11.0 %copy-start = (bf16[3,256,512]{2,1,0:T(8,128)(2,1)S(1)}, bf16[3,256,512]{2,1,0:T(8,128)(2,1)}, u32[]{:S(2)}) copy-start(bf16[3,256,512]{2,1,0:T(8,128)(2,1)} %feat_ref.3) | copy-start | bytes 2359300
  6.5 11.0 %copy-start.1 = (bf16[2,256,512]{2,1,0:T(8,128)(2,1)S(1)}, bf16[2,256,512]{2,1,0:T(8,128)(2,1)}, u32[]{:S(2)}) copy-start(bf16[2,256,512]{2,1,0:T(8,128)(2,1)} %gate_ref.3) | copy-start | bytes 1572868
  6.5 11.0 %copy-start.7 = (f32[512]{0:T(512)S(1)}, f32[512]{0:T(512)}, u32[]{:S(2)}) copy-start(f32[512]{0:T(512)} %param.15) | copy-start | bytes 6148
  6.5 11.0 %copy-start.4 = (f32[3,7,512]{2,1,0:T(8,128)S(1)}, f32[3,7,512]{2,1,0:T(8,128)}, u32[]{:S(2)}) copy-start(f32[3,7,512]{2,1,0:T(8,128)} %short_mr_ref.1) | copy-start | bytes 129028
  6.5 11.0 %copy-start.5 = (f32[3,7,512]{2,1,0:T(8,128)S(1)}, f32[3,7,512]{2,1,0:T(8,128)}, u32[]{:S(2)}) copy-start(f32[3,7,512]{2,1,0:T(8,128)} %short_li_ref.1) | copy-start | bytes 129028
  6.5 11.0 %copy-start.2 = (f32[16,512]{1,0:T(8,128)S(1)}, f32[16,512]{1,0:T(8,128)}, u32[]{:S(2)}) copy-start(f32[16,512]{1,0:T(8,128)} %refs_6_.1) | copy-start | bytes 98308
  6.6 114.8 %all-gather.2.cloned.1.call-start = ((), (), s32[]{:S(2)}) async-start(), calls=%async_computation.2 | async-start | bytes 8650752 | tf_op jit(solution)/shard_map/all_gather | solution.py:388
  9.1 8.4 %collective-permute-start = (bf16[336,512]{1,0:T(8,128)(2,1)}, bf16[336,512]{1,0:T(8,128)(2,1)}, u32[]{:S(2)}, u32[]{:S(2)}) collective-permute-start(bf16[336,512]{1,0:T(8,128)(2,1)} %tails.1), channel_id=1, source_target_pairs={{0,16},{16,32},{32,48},{48,64},{64,80},{80,96},{96,112},{112,128},... | collective-permute-start | bytes 1032200 | tf_op jit(solution)/shard_map/ppermute | solution.py:391
  23.9 13.8 %all-to-all-start = ((f32[4,16,512]{2,1,0:T(8,128)}), f32[4,16,512]{2,1,0:T(8,128)S(1)}, u32[]{:S(2)}, u32[]{:S(2)}) async-start(f32[4,16,512]{2,1,0:T(8,128)} %get-tuple-element.14), calls=%async_computation | async-start | bytes 262144 | tf_op jit(solution)/shard_map/all_to_all | solution.py:398
  31.5 27.8 %copy-start.8 = (s32[2]{0:T(128)}, s32[2]{0:T(128)S(1)}, u32[]{:S(2)}) copy-start(s32[2]{0:T(128)S(1)} %pad_add_fusion.1.refs_0_) | copy-start | bytes 28
  38.3 21.1 %copy-start.6 = (f32[16,512]{1,0:T(8,128)}, f32[16,512]{1,0:T(8,128)S(1)}, u32[]{:S(2)}) copy-start(f32[16,512]{1,0:T(8,128)S(1)} %get-tuple-element.15.refs_4_) | copy-start | bytes 98308
  63.7 57.7 %copy-start.3 = (bf16[256,512]{1,0:T(8,128)(2,1)S(1)}, bf16[256,512]{1,0:T(8,128)(2,1)}, u32[]{:S(2)}) copy-start(bf16[256,512]{1,0:T(8,128)(2,1)} %residual_ref.1) | copy-start | bytes 786436
  63.7 8.4 %collective-permute-start.1 = (bf16[256,512]{1,0:T(8,128)(2,1)}, bf16[256,512]{1,0:T(8,128)(2,1)S(1)}, u32[]{:S(2)}, u32[]{:S(2)}) collective-permute-start(bf16[256,512]{1,0:T(8,128)(2,1)} %close.1), channel_id=1, source_target_pairs={{2,0},{3,1},{4,2},{5,3},{6,4},{7,5},{8,6},{9,7},{10,8},{11,9},{12,... | collective-permute-start | bytes 786440 | tf_op jit(solution)/shard_map/ppermute | solution.py:408
  68.5 8.9 %collective-permute-start.2 = (bf16[256,512]{1,0:T(8,128)(2,1)}, bf16[256,512]{1,0:T(8,128)(2,1)S(1)}, u32[]{:S(2)}, u32[]{:S(2)}) collective-permute-start(bf16[256,512]{1,0:T(8,128)(2,1)} %close.1), channel_id=1, source_target_pairs={{14,0},{15,1},{0,2},{1,3},{2,4},{3,5},{4,6},{5,7},{6,8},{7,9},{8,1... | collective-permute-start | bytes 786440 | tf_op jit(solution)/shard_map/ppermute | solution.py:411
  72.2 8.5 %collective-permute-start.3 = (bf16[256,512]{1,0:T(8,128)(2,1)S(1)}, bf16[256,512]{1,0:T(8,128)(2,1)S(1)}, u32[]{:S(2)}, u32[]{:S(2)}) collective-permute-start(bf16[256,512]{1,0:T(8,128)(2,1)S(1)} %collective-permute-done.1), channel_id=1, source_target_pairs={{2,0},{3,1},{4,2},{5,3},{6,4},{7,5},{8,6},{9,7},{10,8},{11,9},{12,... | collective-permute-start | bytes 786440 | tf_op jit(solution)/shard_map/ppermute | solution.py:408
  77.5 8.8 %collective-permute-start.4 = (bf16[256,512]{1,0:T(8,128)(2,1)S(1)}, bf16[256,512]{1,0:T(8,128)(2,1)S(1)}, u32[]{:S(2)}, u32[]{:S(2)}) collective-permute-start(bf16[256,512]{1,0:T(8,128)(2,1)S(1)} %collective-permute-done.2), channel_id=1, source_target_pairs={{14,0},{15,1},{0,2},{1,3},{2,4},{3,5},{4,6},{5,7},{6,8},{7,9},{8,1... | collective-permute-start | bytes 786440 | tf_op jit(solution)/shard_map/ppermute | solution.py:411
  80.6 9.6 %collective-permute-start.5 = (bf16[256,512]{1,0:T(8,128)(2,1)S(1)}, bf16[256,512]{1,0:T(8,128)(2,1)S(1)}, u32[]{:S(2)}, u32[]{:S(2)}) collective-permute-start(bf16[256,512]{1,0:T(8,128)(2,1)S(1)} %collective-permute-done.3), channel_id=1, source_target_pairs={{2,0},{3,1},{4,2},{5,3},{6,4},{7,5},{8,6},{9,7},{10,8},{11,9},{12,... | collective-permute-start | bytes 786440 | tf_op jit(solution)/shard_map/ppermute | solution.py:408
  86.3 9.7 %collective-permute-start.6 = (bf16[256,512]{1,0:T(8,128)(2,1)S(1)}, bf16[256,512]{1,0:T(8,128)(2,1)S(1)}, u32[]{:S(2)}, u32[]{:S(2)}) collective-permute-start(bf16[256,512]{1,0:T(8,128)(2,1)S(1)} %collective-permute-done.4), channel_id=1, source_target_pairs={{14,0},{15,1},{0,2},{1,3},{2,4},{3,5},{4,6},{5,7},{6,8},{7,9},{8,1... | collective-permute-start | bytes 786440 | tf_op jit(solution)/shard_map/ppermute | solution.py:411
  90.3 10.3 %collective-permute-start.7 = (bf16[256,512]{1,0:T(8,128)(2,1)S(1)}, bf16[256,512]{1,0:T(8,128)(2,1)S(1)}, u32[]{:S(2)}, u32[]{:S(2)}) collective-permute-start(bf16[256,512]{1,0:T(8,128)(2,1)S(1)} %collective-permute-done.5), channel_id=1, source_target_pairs={{2,0},{3,1},{4,2},{5,3},{6,4},{7,5},{8,6},{9,7},{10,8},{11,9},{12,... | collective-permute-start | bytes 786440 | tf_op jit(solution)/shard_map/ppermute | solution.py:408
  100.6 20.8 %copy-start.9 = (bf16[8,256,512]{2,1,0:T(8,128)(2,1)}, bf16[8,256,512]{2,1,0:T(8,128)(2,1)S(1)}, u32[]{:S(2)}) copy-start(bf16[8,256,512]{2,1,0:T(8,128)(2,1)S(1)} %bitcast_dynamic-update-slice_fusion.own_ref) | copy-start | bytes 6291460
  100.6 14.4 %collective-permute-start.8 = (bf16[8,256,512]{2,1,0:T(8,128)(2,1)S(1)}, bf16[8,256,512]{2,1,0:T(8,128)(2,1)}, u32[]{:S(2)}, u32[]{:S(2)}) collective-permute-start(bf16[8,256,512]{2,1,0:T(8,128)(2,1)S(1)} %bitcast_dynamic-update-slice_fusion.own_ref), channel_id=1, source_target_pairs={{0,1},{1,0},{2,3},{3,2},{4,5},{5,4},{6,7},{7,6},{8,9},{9,8},{10,11... | collective-permute-start | bytes 6291464 | tf_op jit(solution)/shard_map/ppermute | solution.py:414
Sparse Core Ops, SparseCore 0:
  10.6 110.8 all-gather.1

commit v4 on v3

--- a/solution.py
+++ b/solution.py
@@ -287,27 +287,27 @@
 
 
 def project_kernel(place_ref, own_ref, other_ref, w_ref, residual_ref, out_ref, y_buf, w_buf, y_sems, w_sems):
-    count = own_ref.shape[0]
+    count, _, depth = own_ref.shape
+    mine = pl.multiple_of(place_ref[1] * depth, depth)
+    theirs = pl.multiple_of((1 - place_ref[1]) * depth, depth)
     copies = []
-    for half, y_ref in enumerate((own_ref, other_ref)):
-        core = place_ref[1] if half == 0 else 1 - place_ref[1]
-        for k in range(count):
-            chip = (place_ref[0] + ORDER[k] + count) % count
-            i = half * count + k
-            copies.append(
-                (
-                    pltpu.make_async_copy(y_ref.at[k], y_buf.at[i], y_sems.at[i]),
-                    pltpu.make_async_copy(w_ref.at[chip, core], w_buf.at[i], w_sems.at[i]),
-                )
+    for k in range(count):
+        chip = (place_ref[0] + ORDER[k] + count) % count
+        copies.append(
+            (
+                pltpu.make_async_copy(own_ref.at[k], y_buf.at[k, :, pl.ds(mine, depth)], y_sems.at[k]),
+                pltpu.make_async_copy(other_ref.at[k], y_buf.at[k, :, pl.ds(theirs, depth)], y_sems.at[count + k]),
+                pltpu.make_async_copy(w_ref.at[chip], w_buf.at[k], w_sems.at[k]),
             )
-    for pair in copies:
-        for copy in pair:
+        )
+    for group in copies:
+        for copy in group:
             copy.start()
     total = residual_ref[...].astype(f32)
-    for i, pair in enumerate(copies):
-        for copy in pair:
+    for k, group in enumerate(copies):
+        for copy in group:
             copy.wait()
-        total += jnp.dot(y_buf[i], w_buf[i], preferred_element_type=f32)
+        total += jnp.dot(y_buf[k], w_buf[k], preferred_element_type=f32)
     out_ref[...] = total.astype(bf16)
 
 
@@ -318,7 +318,7 @@
     hbm = pl.BlockSpec(memory_space=pltpu.HBM)
     arrays = [
         pltpu.with_memory_space_constraint(value, pltpu.HBM)
-        for value in (own, other, w_all.reshape(count, 2, depth, columns))
+        for value in (own, other, w_all.reshape(count, 2 * depth, columns))
     ]
     return pl.pallas_call(
         project_kernel,
@@ -326,10 +326,10 @@
         out_specs=vmem,
         out_shape=jax.ShapeDtypeStruct((tok_rows, columns), bf16),
         scratch_shapes=[
-            pltpu.VMEM((2 * count, tok_rows, depth), bf16),
-            pltpu.VMEM((2 * count, depth, columns), bf16),
+            pltpu.VMEM((count, tok_rows, 2 * depth), bf16),
+            pltpu.VMEM((count, 2 * depth, columns), bf16),
             pltpu.SemaphoreType.DMA((2 * count,)),
-            pltpu.SemaphoreType.DMA((2 * count,)),
+            pltpu.SemaphoreType.DMA((count,)),
         ],
         cost_estimate=pl.CostEstimate(
             flops=4 * count * tok_rows * depth * columns,

time: 135 us -> 135 us (level)
  no operation moved by 1% of the time
where the time goes in v4:
time: 135 us
  starting transfers between devices  49.1 us (36%)
  waiting for transfers between devices  28.3 us (21%)
  blocking collectives  21.1 us (16%)
  Pallas kernels  20.4 us (15%)
  between operations  13.7 us (10%)
  local copies, waits for them, and re-layouts  2.02 us (1%)
    all_to_all x1, blocking collectives, on_device(): lax.all_to_all(total, 'seq', 0, 0, tiled=True, axis_index_groups=far_groups)  21.1 us
    ppermute x4, starting transfers between devices, on_device(): ahead = lax.ppermute(ahead, 'tp', up)  20.6 us
    ppermute x1, starting transfers between devices, on_device(): other = lax.ppermute(own, 'tp', [(t, t ^ 1) for t in range(tp_count)])  10.5 us
    ppermute x4, waiting for transfers between devices, on_device(): ahead = lax.ppermute(ahead, 'tp', up)  8.43 us
    all_to_all x1, starting transfers between devices, on_device(): lax.all_to_all(ends, 'seq', 0, 0, tiled=True, axis_index_groups=near_groups)  7.54 us
    pallas_call x1, Pallas kernels, project(): pl.pallas_call(project_kernel, in_specs=[pl.BlockSpec(memory_space=pltpu....  6.51 us
    pallas_call x1, Pallas kernels, mix(): pl.pallas_call(mix_kernel, grid=(tiles,), in_specs=[pl.BlockSpec((3, tok_...  6.35 us
    all_gather x1, waiting for transfers between devices, on_device(): w_all = lax.all_gather(w_out, 'seq', axis=0, tiled=True)  6.34 us
  transfers between devices with their start and end apart: 11, of which 11 were waited for; matrix products, arithmetic and copies ran while one was open for 2% of the time, Pallas kernels for 10%

profile of v4, /device:TPU:1, one launch (start us, length us, event | category | flops | bytes accessed | tf_op | source)
XLA Modules:
  0.0 134.8 jit_solution(8254195951308220301)
XLA Ops:
  7.3 1.8 %tails.1 = bf16[336,512]{1,0:T(8,128)(2,1)} custom-call(bf16[3,256,512]{2,1,0:T(8,128)(2,1)} %feat_ref.3, bf16[2,256,512]{2,1,0:T(8,128)(2,1)} %gate_ref.3), custom_call_target="tpu_custom_call" | custom-call | tf_op jit(solution)/shard_map/tails/pallas_call | solution.py:364
  9.1 4.7 %collective-permute-start = (bf16[336,512]{1,0:T(8,128)(2,1)}, bf16[336,512]{1,0:T(8,128)(2,1)}, u32[]{:S(2)}, u32[]{:S(2)}) collective-permute-start(bf16[336,512]{1,0:T(8,128)(2,1)} %tails.1), channel_id=1, source_target_pairs={{0,16},{16,32},{32,48},{48,64},{64,80},{80,96},{96,112},{112,128},... | collective-permute-start | bytes 1032200 | tf_op jit(solution)/shard_map/ppermute | solution.py:391
  14.7 0.9 bands.1.band_ref
  15.6 1.9 %collective-permute-done.halo_ref = bf16[336,512]{1,0:T(8,128)(2,1)} collective-permute-done((bf16[336,512]{1,0:T(8,128)(2,1)}, bf16[336,512]{1,0:T(8,128)(2,1)}, u32[]{:S(2)}, u32[]{:S(2)}) %collective-permute-start) | collective-permute-done | bytes 344096 | tf_op jit(solution)/shard_map/ppermute | solution.py:391
  17.6 6.3 %mix.1 = (f32[256,512]{1,0:T(8,128)}, f32[256,512]{1,0:T(8,128)}, f32[128,512]{1,0:T(8,128)}, f32[4,16,512]{2,1,0:T(8,128)}) custom-call(bf16[3,256,512]{2,1,0:T(8,128)(2,1)S(1)} %copy-done, bf16[2,256,512]{2,1,0:T(8,128)(2,1)S(1)} %copy-done.1, bf16[336,512]{1,0:T(8,128)(2,1)} %collective-permute-done.halo_ref, f32[3,7,512]{2,1,0:T(8,128)S(1)} %copy-done.4, ...), custom_call_target="tpu_custom_call" | custom-call | tf_op jit(solution)/shard_map/mix/pallas_call | solution.py:163
  23.9 7.5 %all-to-all-start = ((f32[4,16,512]{2,1,0:T(8,128)}), f32[4,16,512]{2,1,0:T(8,128)S(1)}, u32[]{:S(2)}, u32[]{:S(2)}) async-start(f32[4,16,512]{2,1,0:T(8,128)} %get-tuple-element.14), calls=%async_computation | async-start | bytes 262144 | tf_op jit(solution)/shard_map/all_to_all | solution.py:398
  31.5 6.1 %all-to-all-done.refs_1_ = f32[4,16,512]{2,1,0:T(8,128)S(1)} async-done(((f32[4,16,512]{2,1,0:T(8,128)}), f32[4,16,512]{2,1,0:T(8,128)S(1)}, u32[]{:S(2)}, u32[]{:S(2)}) %all-to-all-start) | async-done | bytes 131104 | tf_op jit(solution)/shard_map/all_to_all | solution.py:398
  38.3 21.1 %all_to_all.10.refs_5_ = f32[8,16,512]{2,1,0:T(8,128)} all-to-all(f32[8,16,512]{2,1,0:T(8,128)S(1)} %get-tuple-element.16), channel_id=1, replica_groups={{0,64,128,192,256,320,384,448},{16,80,144,208,272,336,400,464},{32,96,1..., dimensions={0} | all-to-all | bytes 524288 | tf_op jit(solution)/shard_map/all_to_all | solution.py:400
  59.4 4.3 %close.1 = bf16[256,512]{1,0:T(8,128)(2,1)} custom-call(s32[2]{0:T(128)} %copy-done.8, f32[256,512]{1,0:T(8,128)} %get-tuple-element.11.refs_1_, f32[256,512]{1,0:T(8,128)} %get-tuple-element.12.refs_2_, f32[128,512]{1,0:T(8,128)} %get-tuple-element.13.refs_3_, f32[16,512]{1,0:T(8,128)} %copy-done.6, f32[8,16,512]{2,1,0:T(8,128)} %all_to_all.10.refs_5_, ...), custom_call_target="tpu_custom_call" | custom-call | tf_op jit(solution)/shard_map/close/pallas_call | solution.py:264
  63.7 4.8 %collective-permute-start.1 = (bf16[256,512]{1,0:T(8,128)(2,1)}, bf16[256,512]{1,0:T(8,128)(2,1)S(1)}, u32[]{:S(2)}, u32[]{:S(2)}) collective-permute-start(bf16[256,512]{1,0:T(8,128)(2,1)} %close.1), channel_id=1, source_target_pairs={{2,0},{3,1},{4,2},{5,3},{6,4},{7,5},{8,6},{9,7},{10,8},{11,9},{12,... | collective-permute-start | bytes 786440 | tf_op jit(solution)/shard_map/ppermute | solution.py:408
  68.5 1.9 %collective-permute-start.2 = (bf16[256,512]{1,0:T(8,128)(2,1)}, bf16[256,512]{1,0:T(8,128)(2,1)S(1)}, u32[]{:S(2)}, u32[]{:S(2)}) collective-permute-start(bf16[256,512]{1,0:T(8,128)(2,1)} %close.1), channel_id=1, source_target_pairs={{14,0},{15,1},{0,2},{1,3},{2,4},{3,5},{4,6},{5,7},{6,8},{7,9},{8,1... | collective-permute-start | bytes 786440 | tf_op jit(solution)/shard_map/ppermute | solution.py:411
  70.5 1.0 bitcast_dynamic-update-slice_fusion.7
  72.2 4.9 %collective-permute-start.3 = (bf16[256,512]{1,0:T(8,128)(2,1)S(1)}, bf16[256,512]{1,0:T(8,128)(2,1)S(1)}, u32[]{:S(2)}, u32[]{:S(2)}) collective-permute-start(bf16[256,512]{1,0:T(8,128)(2,1)S(1)} %collective-permute-done.1), channel_id=1, source_target_pairs={{2,0},{3,1},{4,2},{5,3},{6,4},{7,5},{8,6},{9,7},{10,8},{11,9},{12,... | collective-permute-start | bytes 786440 | tf_op jit(solution)/shard_map/ppermute | solution.py:408
  77.5 1.9 %collective-permute-start.4 = (bf16[256,512]{1,0:T(8,128)(2,1)S(1)}, bf16[256,512]{1,0:T(8,128)(2,1)S(1)}, u32[]{:S(2)}, u32[]{:S(2)}) collective-permute-start(bf16[256,512]{1,0:T(8,128)(2,1)S(1)} %collective-permute-done.2), channel_id=1, source_target_pairs={{14,0},{15,1},{0,2},{1,3},{2,4},{3,5},{4,6},{5,7},{6,8},{7,9},{8,1... | collective-permute-start | bytes 786440 | tf_op jit(solution)/shard_map/ppermute | solution.py:411
  79.4 1.2 collective-permute-done.3
  80.6 5.4 %collective-permute-start.5 = (bf16[256,512]{1,0:T(8,128)(2,1)S(1)}, bf16[256,512]{1,0:T(8,128)(2,1)S(1)}, u32[]{:S(2)}, u32[]{:S(2)}) collective-permute-start(bf16[256,512]{1,0:T(8,128)(2,1)S(1)} %collective-permute-done.3), channel_id=1, source_target_pairs={{2,0},{3,1},{4,2},{5,3},{6,4},{7,5},{8,6},{9,7},{10,8},{11,9},{12,... | collective-permute-start | bytes 786440 | tf_op jit(solution)/shard_map/ppermute | solution.py:408
  86.3 1.9 %collective-permute-start.6 = (bf16[256,512]{1,0:T(8,128)(2,1)S(1)}, bf16[256,512]{1,0:T(8,128)(2,1)S(1)}, u32[]{:S(2)}, u32[]{:S(2)}) collective-permute-start(bf16[256,512]{1,0:T(8,128)(2,1)S(1)} %collective-permute-done.4), channel_id=1, source_target_pairs={{14,0},{15,1},{0,2},{1,3},{2,4},{3,5},{4,6},{5,7},{6,8},{7,9},{8,1... | collective-permute-start | bytes 786440 | tf_op jit(solution)/shard_map/ppermute | solution.py:411
  88.3 2.0 %collective-permute-done.5 = bf16[256,512]{1,0:T(8,128)(2,1)S(1)} collective-permute-done((bf16[256,512]{1,0:T(8,128)(2,1)S(1)}, bf16[256,512]{1,0:T(8,128)(2,1)S(1)}, u32[]{:S(2)}, u32[]{:S(2)}) %collective-permute-start.5) | collective-permute-done | bytes 262176 | tf_op jit(solution)/shard_map/ppermute | solution.py:408
  90.3 5.4 %collective-permute-start.7 = (bf16[256,512]{1,0:T(8,128)(2,1)S(1)}, bf16[256,512]{1,0:T(8,128)(2,1)S(1)}, u32[]{:S(2)}, u32[]{:S(2)}) collective-permute-start(bf16[256,512]{1,0:T(8,128)(2,1)S(1)} %collective-permute-done.5), channel_id=1, source_target_pairs={{2,0},{3,1},{4,2},{5,3},{6,4},{7,5},{8,6},{9,7},{10,8},{11,9},{12,... | collective-permute-start | bytes 786440 | tf_op jit(solution)/shard_map/ppermute | solution.py:408
  96.0 4.6 %collective-permute-done.7 = bf16[256,512]{1,0:T(8,128)(2,1)S(1)} collective-permute-done((bf16[256,512]{1,0:T(8,128)(2,1)S(1)}, bf16[256,512]{1,0:T(8,128)(2,1)S(1)}, u32[]{:S(2)}, u32[]{:S(2)}) %collective-permute-start.7) | collective-permute-done | bytes 262176 | tf_op jit(solution)/shard_map/ppermute | solution.py:408
  100.6 10.5 %collective-permute-start.8 = (bf16[8,256,512]{2,1,0:T(8,128)(2,1)S(1)}, bf16[8,256,512]{2,1,0:T(8,128)(2,1)}, u32[]{:S(2)}, u32[]{:S(2)}) collective-permute-start(bf16[8,256,512]{2,1,0:T(8,128)(2,1)S(1)} %bitcast_dynamic-update-slice_fusion.own_ref), channel_id=1, source_target_pairs={{0,1},{1,0},{2,3},{3,2},{4,5},{5,4},{6,7},{7,6},{8,9},{9,8},{10,11... | collective-permute-start | bytes 6291464 | tf_op jit(solution)/shard_map/ppermute | solution.py:414
  111.3 3.8 %collective-permute-done.8.other_ref = bf16[8,256,512]{2,1,0:T(8,128)(2,1)} collective-permute-done((bf16[8,256,512]{2,1,0:T(8,128)(2,1)S(1)}, bf16[8,256,512]{2,1,0:T(8,128)(2,1)}, u32[]{:S(2)}, u32[]{:S(2)}) %collective-permute-start.8) | collective-permute-done | bytes 2097184 | tf_op jit(solution)/shard_map/ppermute | solution.py:414
  115.1 6.3 %all-gather.2.cloned.1.call-done = bf16[8192,512]{1,0:T(8,128)(2,1)} async-done(((bf16[256,512]{1,0:T(8,128)(2,1)}), bf16[8192,512]{1,0:T(8,128)(2,1)}) %all-gather.2.cloned.1.call-update) | async-done | bytes 8388624 | tf_op jit(solution)/shard_map/all_gather | solution.py:388
  121.4 6.5 %project.1 = bf16[256,512]{1,0:T(8,128)(2,1)} custom-call(s32[2]{0:T(128)S(1)} %pad_add_fusion.place_ref, bf16[8,256,512]{2,1,0:T(8,128)(2,1)} %copy-done.9, bf16[8,256,512]{2,1,0:T(8,128)(2,1)} %collective-permute-done.8.other_ref, bf16[8,1024,512]{2,1,0:T(8,128)(2,1)} %bitcast.27, bf16[256,512]{1,0:T(8,128)(2,1)S(1)} %copy-done.3), custom_call_target="tpu_custom_call" | custom-call | flops 2147483648 | bytes 12582912 | tf_op jit(solution)/shard_map/project/pallas_call | solution.py:323
  (41 shorter events, 4.2 us)
Async XLA Ops:
  6.5 11.0 %copy-start = (bf16[3,256,512]{2,1,0:T(8,128)(2,1)S(1)}, bf16[3,256,512]{2,1,0:T(8,128)(2,1)}, u32[]{:S(2)}) copy-start(bf16[3,256,512]{2,1,0:T(8,128)(2,1)} %feat_ref.3) | copy-start | bytes 2359300
  6.5 11.0 %copy-start.1 = (bf16[2,256,512]{2,1,0:T(8,128)(2,1)S(1)}, bf16[2,256,512]{2,1,0:T(8,128)(2,1)}, u32[]{:S(2)}) copy-start(bf16[2,256,512]{2,1,0:T(8,128)(2,1)} %gate_ref.3) | copy-start | bytes 1572868
  6.5 11.0 %copy-start.7 = (f32[512]{0:T(512)S(1)}, f32[512]{0:T(512)}, u32[]{:S(2)}) copy-start(f32[512]{0:T(512)} %param.15) | copy-start | bytes 6148
  6.5 11.0 %copy-start.4 = (f32[3,7,512]{2,1,0:T(8,128)S(1)}, f32[3,7,512]{2,1,0:T(8,128)}, u32[]{:S(2)}) copy-start(f32[3,7,512]{2,1,0:T(8,128)} %short_mr_ref.1) | copy-start | bytes 129028
  6.5 11.0 %copy-start.5 = (f32[3,7,512]{2,1,0:T(8,128)S(1)}, f32[3,7,512]{2,1,0:T(8,128)}, u32[]{:S(2)}) copy-start(f32[3,7,512]{2,1,0:T(8,128)} %short_li_ref.1) | copy-start | bytes 129028
  6.5 11.0 %copy-start.2 = (f32[16,512]{1,0:T(8,128)S(1)}, f32[16,512]{1,0:T(8,128)}, u32[]{:S(2)}) copy-start(f32[16,512]{1,0:T(8,128)} %refs_6_.1) | copy-start | bytes 98308
  6.6 114.8 %all-gather.2.cloned.1.call-start = ((), (), s32[]{:S(2)}) async-start(), calls=%async_computation.2 | async-start | bytes 8650752 | tf_op jit(solution)/shard_map/all_gather | solution.py:388
  9.1 8.4 %collective-permute-start = (bf16[336,512]{1,0:T(8,128)(2,1)}, bf16[336,512]{1,0:T(8,128)(2,1)}, u32[]{:S(2)}, u32[]{:S(2)}) collective-permute-start(bf16[336,512]{1,0:T(8,128)(2,1)} %tails.1), channel_id=1, source_target_pairs={{0,16},{16,32},{32,48},{48,64},{64,80},{80,96},{96,112},{112,128},... | collective-permute-start | bytes 1032200 | tf_op jit(solution)/shard_map/ppermute | solution.py:391
  23.9 13.8 %all-to-all-start = ((f32[4,16,512]{2,1,0:T(8,128)}), f32[4,16,512]{2,1,0:T(8,128)S(1)}, u32[]{:S(2)}, u32[]{:S(2)}) async-start(f32[4,16,512]{2,1,0:T(8,128)} %get-tuple-element.14), calls=%async_computation | async-start | bytes 262144 | tf_op jit(solution)/shard_map/all_to_all | solution.py:398
  31.5 27.8 %copy-start.8 = (s32[2]{0:T(128)}, s32[2]{0:T(128)S(1)}, u32[]{:S(2)}) copy-start(s32[2]{0:T(128)S(1)} %pad_add_fusion.1.refs_0_) | copy-start | bytes 28
  38.3 21.1 %copy-start.6 = (f32[16,512]{1,0:T(8,128)}, f32[16,512]{1,0:T(8,128)S(1)}, u32[]{:S(2)}) copy-start(f32[16,512]{1,0:T(8,128)S(1)} %get-tuple-element.15.refs_4_) | copy-start | bytes 98308
  63.7 57.7 %copy-start.3 = (bf16[256,512]{1,0:T(8,128)(2,1)S(1)}, bf16[256,512]{1,0:T(8,128)(2,1)}, u32[]{:S(2)}) copy-start(bf16[256,512]{1,0:T(8,128)(2,1)} %residual_ref.1) | copy-start | bytes 786436
  63.7 8.4 %collective-permute-start.1 = (bf16[256,512]{1,0:T(8,128)(2,1)}, bf16[256,512]{1,0:T(8,128)(2,1)S(1)}, u32[]{:S(2)}, u32[]{:S(2)}) collective-permute-start(bf16[256,512]{1,0:T(8,128)(2,1)} %close.1), channel_id=1, source_target_pairs={{2,0},{3,1},{4,2},{5,3},{6,4},{7,5},{8,6},{9,7},{10,8},{11,9},{12,... | collective-permute-start | bytes 786440 | tf_op jit(solution)/shard_map/ppermute | solution.py:408
  68.5 8.9 %collective-permute-start.2 = (bf16[256,512]{1,0:T(8,128)(2,1)}, bf16[256,512]{1,0:T(8,128)(2,1)S(1)}, u32[]{:S(2)}, u32[]{:S(2)}) collective-permute-start(bf16[256,512]{1,0:T(8,128)(2,1)} %close.1), channel_id=1, source_target_pairs={{14,0},{15,1},{0,2},{1,3},{2,4},{3,5},{4,6},{5,7},{6,8},{7,9},{8,1... | collective-permute-start | bytes 786440 | tf_op jit(solution)/shard_map/ppermute | solution.py:411
  72.2 8.5 %collective-permute-start.3 = (bf16[256,512]{1,0:T(8,128)(2,1)S(1)}, bf16[256,512]{1,0:T(8,128)(2,1)S(1)}, u32[]{:S(2)}, u32[]{:S(2)}) collective-permute-start(bf16[256,512]{1,0:T(8,128)(2,1)S(1)} %collective-permute-done.1), channel_id=1, source_target_pairs={{2,0},{3,1},{4,2},{5,3},{6,4},{7,5},{8,6},{9,7},{10,8},{11,9},{12,... | collective-permute-start | bytes 786440 | tf_op jit(solution)/shard_map/ppermute | solution.py:408
  77.5 8.8 %collective-permute-start.4 = (bf16[256,512]{1,0:T(8,128)(2,1)S(1)}, bf16[256,512]{1,0:T(8,128)(2,1)S(1)}, u32[]{:S(2)}, u32[]{:S(2)}) collective-permute-start(bf16[256,512]{1,0:T(8,128)(2,1)S(1)} %collective-permute-done.2), channel_id=1, source_target_pairs={{14,0},{15,1},{0,2},{1,3},{2,4},{3,5},{4,6},{5,7},{6,8},{7,9},{8,1... | collective-permute-start | bytes 786440 | tf_op jit(solution)/shard_map/ppermute | solution.py:411
  80.6 9.6 %collective-permute-start.5 = (bf16[256,512]{1,0:T(8,128)(2,1)S(1)}, bf16[256,512]{1,0:T(8,128)(2,1)S(1)}, u32[]{:S(2)}, u32[]{:S(2)}) collective-permute-start(bf16[256,512]{1,0:T(8,128)(2,1)S(1)} %collective-permute-done.3), channel_id=1, source_target_pairs={{2,0},{3,1},{4,2},{5,3},{6,4},{7,5},{8,6},{9,7},{10,8},{11,9},{12,... | collective-permute-start | bytes 786440 | tf_op jit(solution)/shard_map/ppermute | solution.py:408
  86.3 9.7 %collective-permute-start.6 = (bf16[256,512]{1,0:T(8,128)(2,1)S(1)}, bf16[256,512]{1,0:T(8,128)(2,1)S(1)}, u32[]{:S(2)}, u32[]{:S(2)}) collective-permute-start(bf16[256,512]{1,0:T(8,128)(2,1)S(1)} %collective-permute-done.4), channel_id=1, source_target_pairs={{14,0},{15,1},{0,2},{1,3},{2,4},{3,5},{4,6},{5,7},{6,8},{7,9},{8,1... | collective-permute-start | bytes 786440 | tf_op jit(solution)/shard_map/ppermute | solution.py:411
  90.3 10.3 %collective-permute-start.7 = (bf16[256,512]{1,0:T(8,128)(2,1)S(1)}, bf16[256,512]{1,0:T(8,128)(2,1)S(1)}, u32[]{:S(2)}, u32[]{:S(2)}) collective-permute-start(bf16[256,512]{1,0:T(8,128)(2,1)S(1)} %collective-permute-done.5), channel_id=1, source_target_pairs={{2,0},{3,1},{4,2},{5,3},{6,4},{7,5},{8,6},{9,7},{10,8},{11,9},{12,... | collective-permute-start | bytes 786440 | tf_op jit(solution)/shard_map/ppermute | solution.py:408
  100.6 20.8 %copy-start.9 = (bf16[8,256,512]{2,1,0:T(8,128)(2,1)}, bf16[8,256,512]{2,1,0:T(8,128)(2,1)S(1)}, u32[]{:S(2)}) copy-start(bf16[8,256,512]{2,1,0:T(8,128)(2,1)S(1)} %bitcast_dynamic-update-slice_fusion.own_ref) | copy-start | bytes 6291460
  100.6 14.4 %collective-permute-start.8 = (bf16[8,256,512]{2,1,0:T(8,128)(2,1)S(1)}, bf16[8,256,512]{2,1,0:T(8,128)(2,1)}, u32[]{:S(2)}, u32[]{:S(2)}) collective-permute-start(bf16[8,256,512]{2,1,0:T(8,128)(2,1)S(1)} %bitcast_dynamic-update-slice_fusion.own_ref), channel_id=1, source_target_pairs={{0,1},{1,0},{2,3},{3,2},{4,5},{5,4},{6,7},{7,6},{8,9},{9,8},{10,11... | collective-permute-start | bytes 6291464 | tf_op jit(solution)/shard_map/ppermute | solution.py:414
Sparse Core Ops, SparseCore 0:
  10.6 110.8 all-gather.1

commit v5 on v4

--- a/solution.py
+++ b/solution.py
@@ -301,7 +301,7 @@
             )
         )
     for group in copies:
-        for copy in group:
+        for copy in group[::-1]:
             copy.start()
     total = residual_ref[...].astype(f32)
     for k, group in enumerate(copies):

time: 135 us -> 135 us (level)
  no operation moved by 1% of the time
where the time goes in v5:
time: 135 us
  starting transfers between devices  49.1 us (36%)
  waiting for transfers between devices  28.3 us (21%)
  blocking collectives  21.1 us (16%)
  Pallas kernels  20.4 us (15%)
  between operations  13.7 us (10%)
  local copies, waits for them, and re-layouts  2.02 us (1%)
    all_to_all x1, blocking collectives, on_device(): lax.all_to_all(total, 'seq', 0, 0, tiled=True, axis_index_groups=far_groups)  21.1 us
    ppermute x4, starting transfers between devices, on_device(): ahead = lax.ppermute(ahead, 'tp', up)  20.6 us
    ppermute x1, starting transfers between devices, on_device(): other = lax.ppermute(own, 'tp', [(t, t ^ 1) for t in range(tp_count)])  10.5 us
    ppermute x4, waiting for transfers between devices, on_device(): ahead = lax.ppermute(ahead, 'tp', up)  8.43 us
    all_to_all x1, starting transfers between devices, on_device(): lax.all_to_all(ends, 'seq', 0, 0, tiled=True, axis_index_groups=near_groups)  7.54 us
    pallas_call x1, Pallas kernels, project(): pl.pallas_call(project_kernel, in_specs=[pl.BlockSpec(memory_space=pltpu....  6.45 us
    pallas_call x1, Pallas kernels, mix(): pl.pallas_call(mix_kernel, grid=(tiles,), in_specs=[pl.BlockSpec((3, tok_...  6.35 us
    all_gather x1, waiting for transfers between devices, on_device(): w_all = lax.all_gather(w_out, 'seq', axis=0, tiled=True)  6.34 us
  transfers between devices with their start and end apart: 11, of which 11 were waited for; matrix products, arithmetic and copies ran while one was open for 2% of the time, Pallas kernels for 10%

profile of v5, /device:TPU:1, one launch (start us, length us, event | category | flops | bytes accessed | tf_op | source)
XLA Modules:
  0.0 134.7 jit_solution(676652519402238435)
XLA Ops:
  7.3 1.8 %tails.1 = bf16[336,512]{1,0:T(8,128)(2,1)} custom-call(bf16[3,256,512]{2,1,0:T(8,128)(2,1)} %feat_ref.3, bf16[2,256,512]{2,1,0:T(8,128)(2,1)} %gate_ref.3), custom_call_target="tpu_custom_call" | custom-call | tf_op jit(solution)/shard_map/tails/pallas_call | solution.py:364
  9.1 4.7 %collective-permute-start = (bf16[336,512]{1,0:T(8,128)(2,1)}, bf16[336,512]{1,0:T(8,128)(2,1)}, u32[]{:S(2)}, u32[]{:S(2)}) collective-permute-start(bf16[336,512]{1,0:T(8,128)(2,1)} %tails.1), channel_id=1, source_target_pairs={{0,16},{16,32},{32,48},{48,64},{64,80},{80,96},{96,112},{112,128},... | collective-permute-start | bytes 1032200 | tf_op jit(solution)/shard_map/ppermute | solution.py:391
  14.7 0.9 bands.1.band_ref
  15.6 1.9 %collective-permute-done.halo_ref = bf16[336,512]{1,0:T(8,128)(2,1)} collective-permute-done((bf16[336,512]{1,0:T(8,128)(2,1)}, bf16[336,512]{1,0:T(8,128)(2,1)}, u32[]{:S(2)}, u32[]{:S(2)}) %collective-permute-start) | collective-permute-done | bytes 344096 | tf_op jit(solution)/shard_map/ppermute | solution.py:391
  17.6 6.3 %mix.1 = (f32[256,512]{1,0:T(8,128)}, f32[256,512]{1,0:T(8,128)}, f32[128,512]{1,0:T(8,128)}, f32[4,16,512]{2,1,0:T(8,128)}) custom-call(bf16[3,256,512]{2,1,0:T(8,128)(2,1)S(1)} %copy-done, bf16[2,256,512]{2,1,0:T(8,128)(2,1)S(1)} %copy-done.1, bf16[336,512]{1,0:T(8,128)(2,1)} %collective-permute-done.halo_ref, f32[3,7,512]{2,1,0:T(8,128)S(1)} %copy-done.4, ...), custom_call_target="tpu_custom_call" | custom-call | tf_op jit(solution)/shard_map/mix/pallas_call | solution.py:163
  23.9 7.5 %all-to-all-start = ((f32[4,16,512]{2,1,0:T(8,128)}), f32[4,16,512]{2,1,0:T(8,128)S(1)}, u32[]{:S(2)}, u32[]{:S(2)}) async-start(f32[4,16,512]{2,1,0:T(8,128)} %get-tuple-element.14), calls=%async_computation | async-start | bytes 262144 | tf_op jit(solution)/shard_map/all_to_all | solution.py:398
  31.5 6.1 %all-to-all-done.refs_1_ = f32[4,16,512]{2,1,0:T(8,128)S(1)} async-done(((f32[4,16,512]{2,1,0:T(8,128)}), f32[4,16,512]{2,1,0:T(8,128)S(1)}, u32[]{:S(2)}, u32[]{:S(2)}) %all-to-all-start) | async-done | bytes 131104 | tf_op jit(solution)/shard_map/all_to_all | solution.py:398
  38.3 21.1 %all_to_all.10.refs_5_ = f32[8,16,512]{2,1,0:T(8,128)} all-to-all(f32[8,16,512]{2,1,0:T(8,128)S(1)} %get-tuple-element.16), channel_id=1, replica_groups={{0,64,128,192,256,320,384,448},{16,80,144,208,272,336,400,464},{32,96,1..., dimensions={0} | all-to-all | bytes 524288 | tf_op jit(solution)/shard_map/all_to_all | solution.py:400
  59.4 4.3 %close.1 = bf16[256,512]{1,0:T(8,128)(2,1)} custom-call(s32[2]{0:T(128)} %copy-done.8, f32[256,512]{1,0:T(8,128)} %get-tuple-element.11.refs_1_, f32[256,512]{1,0:T(8,128)} %get-tuple-element.12.refs_2_, f32[128,512]{1,0:T(8,128)} %get-tuple-element.13.refs_3_, f32[16,512]{1,0:T(8,128)} %copy-done.6, f32[8,16,512]{2,1,0:T(8,128)} %all_to_all.10.refs_5_, ...), custom_call_target="tpu_custom_call" | custom-call | tf_op jit(solution)/shard_map/close/pallas_call | solution.py:264
  63.7 4.8 %collective-permute-start.1 = (bf16[256,512]{1,0:T(8,128)(2,1)}, bf16[256,512]{1,0:T(8,128)(2,1)S(1)}, u32[]{:S(2)}, u32[]{:S(2)}) collective-permute-start(bf16[256,512]{1,0:T(8,128)(2,1)} %close.1), channel_id=1, source_target_pairs={{2,0},{3,1},{4,2},{5,3},{6,4},{7,5},{8,6},{9,7},{10,8},{11,9},{12,... | collective-permute-start | bytes 786440 | tf_op jit(solution)/shard_map/ppermute | solution.py:408
  68.5 1.9 %collective-permute-start.2 = (bf16[256,512]{1,0:T(8,128)(2,1)}, bf16[256,512]{1,0:T(8,128)(2,1)S(1)}, u32[]{:S(2)}, u32[]{:S(2)}) collective-permute-start(bf16[256,512]{1,0:T(8,128)(2,1)} %close.1), channel_id=1, source_target_pairs={{14,0},{15,1},{0,2},{1,3},{2,4},{3,5},{4,6},{5,7},{6,8},{7,9},{8,1... | collective-permute-start | bytes 786440 | tf_op jit(solution)/shard_map/ppermute | solution.py:411
  70.5 1.0 bitcast_dynamic-update-slice_fusion.7
  72.2 4.9 %collective-permute-start.3 = (bf16[256,512]{1,0:T(8,128)(2,1)S(1)}, bf16[256,512]{1,0:T(8,128)(2,1)S(1)}, u32[]{:S(2)}, u32[]{:S(2)}) collective-permute-start(bf16[256,512]{1,0:T(8,128)(2,1)S(1)} %collective-permute-done.1), channel_id=1, source_target_pairs={{2,0},{3,1},{4,2},{5,3},{6,4},{7,5},{8,6},{9,7},{10,8},{11,9},{12,... | collective-permute-start | bytes 786440 | tf_op jit(solution)/shard_map/ppermute | solution.py:408
  77.5 1.9 %collective-permute-start.4 = (bf16[256,512]{1,0:T(8,128)(2,1)S(1)}, bf16[256,512]{1,0:T(8,128)(2,1)S(1)}, u32[]{:S(2)}, u32[]{:S(2)}) collective-permute-start(bf16[256,512]{1,0:T(8,128)(2,1)S(1)} %collective-permute-done.2), channel_id=1, source_target_pairs={{14,0},{15,1},{0,2},{1,3},{2,4},{3,5},{4,6},{5,7},{6,8},{7,9},{8,1... | collective-permute-start | bytes 786440 | tf_op jit(solution)/shard_map/ppermute | solution.py:411
  79.4 1.2 collective-permute-done.3
  80.6 5.4 %collective-permute-start.5 = (bf16[256,512]{1,0:T(8,128)(2,1)S(1)}, bf16[256,512]{1,0:T(8,128)(2,1)S(1)}, u32[]{:S(2)}, u32[]{:S(2)}) collective-permute-start(bf16[256,512]{1,0:T(8,128)(2,1)S(1)} %collective-permute-done.3), channel_id=1, source_target_pairs={{2,0},{3,1},{4,2},{5,3},{6,4},{7,5},{8,6},{9,7},{10,8},{11,9},{12,... | collective-permute-start | bytes 786440 | tf_op jit(solution)/shard_map/ppermute | solution.py:408
  86.3 1.9 %collective-permute-start.6 = (bf16[256,512]{1,0:T(8,128)(2,1)S(1)}, bf16[256,512]{1,0:T(8,128)(2,1)S(1)}, u32[]{:S(2)}, u32[]{:S(2)}) collective-permute-start(bf16[256,512]{1,0:T(8,128)(2,1)S(1)} %collective-permute-done.4), channel_id=1, source_target_pairs={{14,0},{15,1},{0,2},{1,3},{2,4},{3,5},{4,6},{5,7},{6,8},{7,9},{8,1... | collective-permute-start | bytes 786440 | tf_op jit(solution)/shard_map/ppermute | solution.py:411
  88.3 2.0 %collective-permute-done.5 = bf16[256,512]{1,0:T(8,128)(2,1)S(1)} collective-permute-done((bf16[256,512]{1,0:T(8,128)(2,1)S(1)}, bf16[256,512]{1,0:T(8,128)(2,1)S(1)}, u32[]{:S(2)}, u32[]{:S(2)}) %collective-permute-start.5) | collective-permute-done | bytes 262176 | tf_op jit(solution)/shard_map/ppermute | solution.py:408
  90.3 5.4 %collective-permute-start.7 = (bf16[256,512]{1,0:T(8,128)(2,1)S(1)}, bf16[256,512]{1,0:T(8,128)(2,1)S(1)}, u32[]{:S(2)}, u32[]{:S(2)}) collective-permute-start(bf16[256,512]{1,0:T(8,128)(2,1)S(1)} %collective-permute-done.5), channel_id=1, source_target_pairs={{2,0},{3,1},{4,2},{5,3},{6,4},{7,5},{8,6},{9,7},{10,8},{11,9},{12,... | collective-permute-start | bytes 786440 | tf_op jit(solution)/shard_map/ppermute | solution.py:408
  96.0 4.6 %collective-permute-done.7 = bf16[256,512]{1,0:T(8,128)(2,1)S(1)} collective-permute-done((bf16[256,512]{1,0:T(8,128)(2,1)S(1)}, bf16[256,512]{1,0:T(8,128)(2,1)S(1)}, u32[]{:S(2)}, u32[]{:S(2)}) %collective-permute-start.7) | collective-permute-done | bytes 262176 | tf_op jit(solution)/shard_map/ppermute | solution.py:408
  100.6 10.5 %collective-permute-start.8 = (bf16[8,256,512]{2,1,0:T(8,128)(2,1)S(1)}, bf16[8,256,512]{2,1,0:T(8,128)(2,1)}, u32[]{:S(2)}, u32[]{:S(2)}) collective-permute-start(bf16[8,256,512]{2,1,0:T(8,128)(2,1)S(1)} %bitcast_dynamic-update-slice_fusion.own_ref), channel_id=1, source_target_pairs={{0,1},{1,0},{2,3},{3,2},{4,5},{5,4},{6,7},{7,6},{8,9},{9,8},{10,11... | collective-permute-start | bytes 6291464 | tf_op jit(solution)/shard_map/ppermute | solution.py:414
  111.3 3.8 %collective-permute-done.8.other_ref = bf16[8,256,512]{2,1,0:T(8,128)(2,1)} collective-permute-done((bf16[8,256,512]{2,1,0:T(8,128)(2,1)S(1)}, bf16[8,256,512]{2,1,0:T(8,128)(2,1)}, u32[]{:S(2)}, u32[]{:S(2)}) %collective-permute-start.8) | collective-permute-done | bytes 2097184 | tf_op jit(solution)/shard_map/ppermute | solution.py:414
  115.1 6.3 %all-gather.2.cloned.1.call-done = bf16[8192,512]{1,0:T(8,128)(2,1)} async-done(((bf16[256,512]{1,0:T(8,128)(2,1)}), bf16[8192,512]{1,0:T(8,128)(2,1)}) %all-gather.2.cloned.1.call-update) | async-done | bytes 8388624 | tf_op jit(solution)/shard_map/all_gather | solution.py:388
  121.4 6.5 %project.1 = bf16[256,512]{1,0:T(8,128)(2,1)} custom-call(s32[2]{0:T(128)S(1)} %pad_add_fusion.place_ref, bf16[8,256,512]{2,1,0:T(8,128)(2,1)} %copy-done.9, bf16[8,256,512]{2,1,0:T(8,128)(2,1)} %collective-permute-done.8.other_ref, bf16[8,1024,512]{2,1,0:T(8,128)(2,1)} %bitcast.27, bf16[256,512]{1,0:T(8,128)(2,1)S(1)} %copy-done.3), custom_call_target="tpu_custom_call" | custom-call | flops 2147483648 | bytes 12582912 | tf_op jit(solution)/shard_map/project/pallas_call | solution.py:323
  (41 shorter events, 4.2 us)
Async XLA Ops:
  6.5 11.0 %copy-start = (bf16[3,256,512]{2,1,0:T(8,128)(2,1)S(1)}, bf16[3,256,512]{2,1,0:T(8,128)(2,1)}, u32[]{:S(2)}) copy-start(bf16[3,256,512]{2,1,0:T(8,128)(2,1)} %feat_ref.3) | copy-start | bytes 2359300
  6.5 11.0 %copy-start.1 = (bf16[2,256,512]{2,1,0:T(8,128)(2,1)S(1)}, bf16[2,256,512]{2,1,0:T(8,128)(2,1)}, u32[]{:S(2)}) copy-start(bf16[2,256,512]{2,1,0:T(8,128)(2,1)} %gate_ref.3) | copy-start | bytes 1572868
  6.5 11.0 %copy-start.7 = (f32[512]{0:T(512)S(1)}, f32[512]{0:T(512)}, u32[]{:S(2)}) copy-start(f32[512]{0:T(512)} %param.15) | copy-start | bytes 6148
  6.5 11.0 %copy-start.4 = (f32[3,7,512]{2,1,0:T(8,128)S(1)}, f32[3,7,512]{2,1,0:T(8,128)}, u32[]{:S(2)}) copy-start(f32[3,7,512]{2,1,0:T(8,128)} %short_mr_ref.1) | copy-start | bytes 129028
  6.5 11.0 %copy-start.5 = (f32[3,7,512]{2,1,0:T(8,128)S(1)}, f32[3,7,512]{2,1,0:T(8,128)}, u32[]{:S(2)}) copy-start(f32[3,7,512]{2,1,0:T(8,128)} %short_li_ref.1) | copy-start | bytes 129028
  6.5 11.0 %copy-start.2 = (f32[16,512]{1,0:T(8,128)S(1)}, f32[16,512]{1,0:T(8,128)}, u32[]{:S(2)}) copy-start(f32[16,512]{1,0:T(8,128)} %refs_6_.1) | copy-start | bytes 98308
  6.6 114.8 %all-gather.2.cloned.1.call-start = ((), (), s32[]{:S(2)}) async-start(), calls=%async_computation.2 | async-start | bytes 8650752 | tf_op jit(solution)/shard_map/all_gather | solution.py:388
  9.1 8.4 %collective-permute-start = (bf16[336,512]{1,0:T(8,128)(2,1)}, bf16[336,512]{1,0:T(8,128)(2,1)}, u32[]{:S(2)}, u32[]{:S(2)}) collective-permute-start(bf16[336,512]{1,0:T(8,128)(2,1)} %tails.1), channel_id=1, source_target_pairs={{0,16},{16,32},{32,48},{48,64},{64,80},{80,96},{96,112},{112,128},... | collective-permute-start | bytes 1032200 | tf_op jit(solution)/shard_map/ppermute | solution.py:391
  23.9 13.8 %all-to-all-start = ((f32[4,16,512]{2,1,0:T(8,128)}), f32[4,16,512]{2,1,0:T(8,128)S(1)}, u32[]{:S(2)}, u32[]{:S(2)}) async-start(f32[4,16,512]{2,1,0:T(8,128)} %get-tuple-element.14), calls=%async_computation | async-start | bytes 262144 | tf_op jit(solution)/shard_map/all_to_all | solution.py:398
  31.5 27.8 %copy-start.8 = (s32[2]{0:T(128)}, s32[2]{0:T(128)S(1)}, u32[]{:S(2)}) copy-start(s32[2]{0:T(128)S(1)} %pad_add_fusion.1.refs_0_) | copy-start | bytes 28
  38.3 21.1 %copy-start.6 = (f32[16,512]{1,0:T(8,128)}, f32[16,512]{1,0:T(8,128)S(1)}, u32[]{:S(2)}) copy-start(f32[16,512]{1,0:T(8,128)S(1)} %get-tuple-element.15.refs_4_) | copy-start | bytes 98308
  63.7 57.7 %copy-start.3 = (bf16[256,512]{1,0:T(8,128)(2,1)S(1)}, bf16[256,512]{1,0:T(8,128)(2,1)}, u32[]{:S(2)}) copy-start(bf16[256,512]{1,0:T(8,128)(2,1)} %residual_ref.1) | copy-start | bytes 786436
  63.7 8.4 %collective-permute-start.1 = (bf16[256,512]{1,0:T(8,128)(2,1)}, bf16[256,512]{1,0:T(8,128)(2,1)S(1)}, u32[]{:S(2)}, u32[]{:S(2)}) collective-permute-start(bf16[256,512]{1,0:T(8,128)(2,1)} %close.1), channel_id=1, source_target_pairs={{2,0},{3,1},{4,2},{5,3},{6,4},{7,5},{8,6},{9,7},{10,8},{11,9},{12,... | collective-permute-start | bytes 786440 | tf_op jit(solution)/shard_map/ppermute | solution.py:408
  68.5 8.9 %collective-permute-start.2 = (bf16[256,512]{1,0:T(8,128)(2,1)}, bf16[256,512]{1,0:T(8,128)(2,1)S(1)}, u32[]{:S(2)}, u32[]{:S(2)}) collective-permute-start(bf16[256,512]{1,0:T(8,128)(2,1)} %close.1), channel_id=1, source_target_pairs={{14,0},{15,1},{0,2},{1,3},{2,4},{3,5},{4,6},{5,7},{6,8},{7,9},{8,1... | collective-permute-start | bytes 786440 | tf_op jit(solution)/shard_map/ppermute | solution.py:411
  72.2 8.5 %collective-permute-start.3 = (bf16[256,512]{1,0:T(8,128)(2,1)S(1)}, bf16[256,512]{1,0:T(8,128)(2,1)S(1)}, u32[]{:S(2)}, u32[]{:S(2)}) collective-permute-start(bf16[256,512]{1,0:T(8,128)(2,1)S(1)} %collective-permute-done.1), channel_id=1, source_target_pairs={{2,0},{3,1},{4,2},{5,3},{6,4},{7,5},{8,6},{9,7},{10,8},{11,9},{12,... | collective-permute-start | bytes 786440 | tf_op jit(solution)/shard_map/ppermute | solution.py:408
  77.5 8.8 %collective-permute-start.4 = (bf16[256,512]{1,0:T(8,128)(2,1)S(1)}, bf16[256,512]{1,0:T(8,128)(2,1)S(1)}, u32[]{:S(2)}, u32[]{:S(2)}) collective-permute-start(bf16[256,512]{1,0:T(8,128)(2,1)S(1)} %collective-permute-done.2), channel_id=1, source_target_pairs={{14,0},{15,1},{0,2},{1,3},{2,4},{3,5},{4,6},{5,7},{6,8},{7,9},{8,1... | collective-permute-start | bytes 786440 | tf_op jit(solution)/shard_map/ppermute | solution.py:411
  80.6 9.6 %collective-permute-start.5 = (bf16[256,512]{1,0:T(8,128)(2,1)S(1)}, bf16[256,512]{1,0:T(8,128)(2,1)S(1)}, u32[]{:S(2)}, u32[]{:S(2)}) collective-permute-start(bf16[256,512]{1,0:T(8,128)(2,1)S(1)} %collective-permute-done.3), channel_id=1, source_target_pairs={{2,0},{3,1},{4,2},{5,3},{6,4},{7,5},{8,6},{9,7},{10,8},{11,9},{12,... | collective-permute-start | bytes 786440 | tf_op jit(solution)/shard_map/ppermute | solution.py:408
  86.3 9.7 %collective-permute-start.6 = (bf16[256,512]{1,0:T(8,128)(2,1)S(1)}, bf16[256,512]{1,0:T(8,128)(2,1)S(1)}, u32[]{:S(2)}, u32[]{:S(2)}) collective-permute-start(bf16[256,512]{1,0:T(8,128)(2,1)S(1)} %collective-permute-done.4), channel_id=1, source_target_pairs={{14,0},{15,1},{0,2},{1,3},{2,4},{3,5},{4,6},{5,7},{6,8},{7,9},{8,1... | collective-permute-start | bytes 786440 | tf_op jit(solution)/shard_map/ppermute | solution.py:411
  90.3 10.3 %collective-permute-start.7 = (bf16[256,512]{1,0:T(8,128)(2,1)S(1)}, bf16[256,512]{1,0:T(8,128)(2,1)S(1)}, u32[]{:S(2)}, u32[]{:S(2)}) collective-permute-start(bf16[256,512]{1,0:T(8,128)(2,1)S(1)} %collective-permute-done.5), channel_id=1, source_target_pairs={{2,0},{3,1},{4,2},{5,3},{6,4},{7,5},{8,6},{9,7},{10,8},{11,9},{12,... | collective-permute-start | bytes 786440 | tf_op jit(solution)/shard_map/ppermute | solution.py:408
  100.6 20.8 %copy-start.9 = (bf16[8,256,512]{2,1,0:T(8,128)(2,1)}, bf16[8,256,512]{2,1,0:T(8,128)(2,1)S(1)}, u32[]{:S(2)}) copy-start(bf16[8,256,512]{2,1,0:T(8,128)(2,1)S(1)} %bitcast_dynamic-update-slice_fusion.own_ref) | copy-start | bytes 6291460
  100.6 14.4 %collective-permute-start.8 = (bf16[8,256,512]{2,1,0:T(8,128)(2,1)S(1)}, bf16[8,256,512]{2,1,0:T(8,128)(2,1)}, u32[]{:S(2)}, u32[]{:S(2)}) collective-permute-start(bf16[8,256,512]{2,1,0:T(8,128)(2,1)S(1)} %bitcast_dynamic-update-slice_fusion.own_ref), channel_id=1, source_target_pairs={{0,1},{1,0},{2,3},{3,2},{4,5},{5,4},{6,7},{7,6},{8,9},{9,8},{10,11... | collective-permute-start | bytes 6291464 | tf_op jit(solution)/shard_map/ppermute | solution.py:414
Sparse Core Ops, SparseCore 0:
  10.6 110.8 all-gather.1
